TPU v7x, 128 devices: a whole 4x4x4 slice. The times are simulated.
128 devices in a mesh: ctx: 8 (over z, core), ch: 16 (over x, y).
Axes of the slice: x: 4, y: 4, z: 4, core: 2. Of those that a mesh axis runs over, the one named last changes fastest.
Arguments:
- out_gate: bfloat16 [1024, 4096], P('ctx', 'ch'), may hold values from -6 to 6
- in_gate: bfloat16 [1024, 4096], P('ctx', 'ch'), may hold values from -6 to 6
- signal: bfloat16 [1024, 4096], P('ctx', 'ch'), may hold values from -6 to 6
- cotangent: bfloat16 [1024, 4096], P('ctx', 'ch'), may hold values from -6 to 6
- filters: float32 [1024, 256], P('ctx', 'ch'), may hold values from -0.1875 to 0.1875
- block_ids: int32 [16], P('ctx'), may hold values from 0 to 15, each once
Outputs:
- outer_grad: bfloat16 [1024, 4096], P('ctx', 'ch')
- inner_grad: bfloat16 [1024, 4096], P('ctx', 'ch')
- signal_grad: bfloat16 [1024, 4096], P('ctx', 'ch')
- filter_grad: float32 [1024, 256], P('ctx', 'ch')
Inputs may be any that keep to these rules, and one draw needn't show every extreme that they name: block_ids is a permutation of the context blocks.
All inputs are finite; a program needn't handle non-finite values.
Results may differ from a plain program's by a relative error of at most 0.005.
Values may be sent and summed in bfloat16 or wider, within the bound.
A program may use at most 64 MiB of HBM per device.

v0:
```python
from functools import partial

import jax
import jax.numpy as jnp
from jax import lax
from jax.sharding import PartitionSpec as P

exact_mode = lax.Precision.HIGHEST


def factor_pair(total):
    first = 2
    for candidate in range(2, total + 1, 2):
        if total % candidate == 0 and candidate * candidate <= total:
            first = candidate
    return (first, total // first)


def trig_table(rows, cols, period):
    left = jnp.arange(rows, dtype=jnp.int32)
    right = jnp.arange(cols, dtype=jnp.int32)
    turns = left[:, None] * right[None, :] % period
    angle = turns.astype(jnp.float32) * (2.0 * jnp.pi / period)
    return (jnp.cos(angle), jnp.sin(angle))


def forward(values, total, suffix):
    first, second = factor_pair(total)
    used = values.shape[1] // second
    leading = values.shape[:1]
    trailing = values.shape[2:]
    shaped = values.reshape(leading + (used, second) + trailing)
    cos_one, sin_one = trig_table(first, used, first)
    section_one = "kn,pnm" + suffix + "->pkm" + suffix
    a_re = jnp.einsum(section_one, cos_one, shaped, precision=exact_mode)
    a_im = -jnp.einsum(section_one, sin_one, shaped, precision=exact_mode)
    tw_cos, tw_sin = trig_table(first, second, total)
    tw_cos = tw_cos.reshape((first, second) + (1,) * len(trailing))
    tw_sin = tw_sin.reshape((first, second) + (1,) * len(trailing))
    b_re = a_re * tw_cos + a_im * tw_sin
    b_im = a_im * tw_cos - a_re * tw_sin
    cos_two, sin_two = trig_table(second, second, second)
    section_two = "jm,pkm" + suffix + "->pjk" + suffix
    x_re = jnp.einsum(section_two, cos_two, b_re, precision=exact_mode) + jnp.einsum(
        section_two, sin_two, b_im, precision=exact_mode
    )
    x_im = jnp.einsum(section_two, cos_two, b_im, precision=exact_mode) - jnp.einsum(
        section_two, sin_two, b_re, precision=exact_mode
    )
    return (
        x_re.reshape(leading + (total,) + trailing),
        x_im.reshape(leading + (total,) + trailing),
    )


def inverse(x_re, x_im, total, keep, suffix):
    first, second = factor_pair(total)
    leading = x_re.shape[:1]
    trailing = x_re.shape[2:]
    spec_re = x_re.reshape(leading + (second, first) + trailing)
    spec_im = x_im.reshape(leading + (second, first) + trailing)
    cos_two, sin_two = trig_table(second, second, second)
    section_a = "mj,pjk" + suffix + "->pkm" + suffix
    y_re = jnp.einsum(section_a, cos_two, spec_re, precision=exact_mode) - jnp.einsum(
        section_a, sin_two, spec_im, precision=exact_mode
    )
    y_im = jnp.einsum(section_a, cos_two, spec_im, precision=exact_mode) + jnp.einsum(
        section_a, sin_two, spec_re, precision=exact_mode
    )
    tw_cos, tw_sin = trig_table(first, second, total)
    tw_cos = tw_cos.reshape((first, second) + (1,) * len(trailing))
    tw_sin = tw_sin.reshape((first, second) + (1,) * len(trailing))
    z_re = y_re * tw_cos - y_im * tw_sin
    z_im = y_re * tw_sin + y_im * tw_cos
    used = keep // second
    cos_one, sin_one = trig_table(used, first, first)
    section_b = "nk,pkm" + suffix + "->pnm" + suffix
    result = jnp.einsum(section_b, cos_one, z_re, precision=exact_mode) - jnp.einsum(
        section_b, sin_one, z_im, precision=exact_mode
    )
    return result.reshape(leading + (keep,) + trailing) / total


def unchanged(state):
    return state


def ahead_terms(state, slot, level, u_re, u_im, lag_re, lag_im, lg_re, lg_im):
    z_re, z_im, d_re, d_im, s_re, s_im = state
    f_re = lax.dynamic_index_in_dim(lag_re, level, 0, keepdims=False)
    f_im = lax.dynamic_index_in_dim(lag_im, level, 0, keepdims=False)
    z_re = z_re.at[slot].add(f_re * u_re - f_im * u_im)
    z_im = z_im.at[slot].add(f_re * u_im + f_im * u_re)
    cross_re = lg_re[slot] * u_re + lg_im[slot] * u_im
    cross_im = lg_im[slot] * u_re - lg_re[slot] * u_im
    old_re = lax.dynamic_index_in_dim(s_re, level, 0, keepdims=False)
    old_im = lax.dynamic_index_in_dim(s_im, level, 0, keepdims=False)
    s_re = lax.dynamic_update_index_in_dim(s_re, old_re + cross_re, level, 0)
    s_im = lax.dynamic_update_index_in_dim(s_im, old_im + cross_im, level, 0)
    return (z_re, z_im, d_re, d_im, s_re, s_im)


def behind_terms(state, slot, level, g_re, g_im, lag_re, lag_im):
    z_re, z_im, d_re, d_im, s_re, s_im = state
    f_re = lax.dynamic_index_in_dim(lag_re, level, 0, keepdims=False)
    f_im = lax.dynamic_index_in_dim(lag_im, level, 0, keepdims=False)
    d_re = d_re.at[slot].add(f_re * g_re + f_im * g_im)
    d_im = d_im.at[slot].add(f_re * g_im - f_im * g_re)
    return (z_re, z_im, d_re, d_im, s_re, s_im)


def pair_sums(product, weighted, kernel, local_ids, span, nblk, repeat):
    total = 2 * span
    width = product.shape[1]
    groups = kernel.shape[1]
    slots = local_ids.shape[0]
    lag_blocks = kernel.reshape(nblk, span, groups)
    earlier = jnp.concatenate([jnp.zeros((1, span, groups), jnp.float32), lag_blocks[:-1]], axis=0)
    segments = jnp.concatenate([lag_blocks, earlier], axis=1)
    lag_re, lag_im = forward(segments, total, "w")
    lag_re = jnp.tile(lag_re, (1, 1, repeat))
    lag_im = jnp.tile(lag_im, (1, 1, repeat))
    prod_blocks = product.reshape(slots, span, width)
    weight_blocks = weighted.reshape(slots, span, width)
    lg_re, lg_im = forward(weight_blocks.astype(jnp.float32), total, "w")
    pair_zero = jnp.zeros((slots, total, width), jnp.float32)
    lag_zero = jnp.zeros((nblk, total, width), jnp.float32)
    start_carry = (pair_zero, pair_zero, pair_zero, pair_zero, lag_zero, lag_zero)
    piece_prod = lax.all_gather(prod_blocks, "ctx", axis=0, tiled=True)
    piece_weight = lax.all_gather(weight_blocks, "ctx", axis=0, tiled=True)
    piece_ids = lax.all_gather(local_ids, "ctx", axis=0, tiled=True)
    pu_re, pu_im = forward(piece_prod.astype(jnp.float32), total, "w")
    pg_re, pg_im = forward(piece_weight.astype(jnp.float32), total, "w")

    def one_block(index, state):
        u_re = lax.dynamic_index_in_dim(pu_re, index, 0, keepdims=False)
        u_im = lax.dynamic_index_in_dim(pu_im, index, 0, keepdims=False)
        g_re = lax.dynamic_index_in_dim(pg_re, index, 0, keepdims=False)
        g_im = lax.dynamic_index_in_dim(pg_im, index, 0, keepdims=False)
        source = lax.dynamic_index_in_dim(piece_ids, index, 0, keepdims=False)
        for slot in range(slots):
            offset = local_ids[slot] - source
            ahead_at = jnp.clip(offset, 0, nblk - 1).astype(jnp.int32)
            behind_at = jnp.clip(-offset, 0, nblk - 1).astype(jnp.int32)
            state = lax.cond(
                offset >= 0,
                partial(
                    ahead_terms,
                    slot=slot,
                    level=ahead_at,
                    u_re=u_re,
                    u_im=u_im,
                    lag_re=lag_re,
                    lag_im=lag_im,
                    lg_re=lg_re,
                    lg_im=lg_im,
                ),
                unchanged,
                state,
            )
            state = lax.cond(
                offset <= 0,
                partial(
                    behind_terms,
                    slot=slot,
                    level=behind_at,
                    g_re=g_re,
                    g_im=g_im,
                    lag_re=lag_re,
                    lag_im=lag_im,
                ),
                unchanged,
                state,
            )
        return state

    totals = lax.fori_loop(0, piece_ids.shape[0], one_block, start_carry)
    z_re, z_im, d_re, d_im, s_re, s_im = totals
    conv = inverse(z_re, z_im, total, span, "w").reshape(slots * span, width)
    back = inverse(d_re, d_im, total, span, "w").reshape(slots * span, width)
    rotated = inverse(s_re, s_im, total, total, "w")
    shifted = jnp.concatenate(
        [rotated[1:, span:], jnp.zeros((1, span, width), jnp.float32)], axis=0
    )
    per_channel = rotated[:, :span] + shifted
    per_filter = jnp.sum(per_channel.reshape(nblk, span, repeat, groups), axis=2)
    return (conv, back, per_filter)


def local(out_gate, in_gate, signal, cotangent, filters, block_ids):
    span = out_gate.shape[0] // 2
    width = out_gate.shape[1]
    lag_cols = lax.all_gather(filters, "ctx", axis=0, tiled=True)
    kernel = lax.all_gather(lag_cols, "ch", axis=1, tiled=True)
    length, groups = kernel.shape
    nblk = length // span
    repeat = width // groups
    product = (in_gate.astype(jnp.float32) * signal.astype(jnp.float32)).astype(jnp.bfloat16)
    weighted = (cotangent.astype(jnp.float32) * out_gate.astype(jnp.float32)).astype(jnp.bfloat16)
    conv, back, per_filter = pair_sums(product, weighted, kernel, block_ids, span, nblk, repeat)
    outer_grad = (cotangent.astype(jnp.float32) * conv).astype(jnp.bfloat16)
    inner_grad = (back * signal.astype(jnp.float32)).astype(jnp.bfloat16)
    signal_grad = (back * in_gate.astype(jnp.float32)).astype(jnp.bfloat16)
    partial_sum = lax.psum_scatter(per_filter, "ch", scatter_dimension=2, tiled=True)
    owned = lax.psum_scatter(partial_sum, "ctx", scatter_dimension=0, tiled=True)
    filter_grad = owned.reshape(owned.shape[0] * owned.shape[1], owned.shape[2])
    return (outer_grad, inner_grad, signal_grad, filter_grad)


def solution(mesh):
    return jax.shard_map(
        local,
        mesh=mesh,
        in_specs=(
            P("ctx", "ch"),
            P("ctx", "ch"),
            P("ctx", "ch"),
            P("ctx", "ch"),
            P("ctx", "ch"),
            P("ctx"),
        ),
        out_specs=(P("ctx", "ch"), P("ctx", "ch"), P("ctx", "ch"), P("ctx", "ch")),
        check_vma=False,
    )
```

profile of v0, /device:TPU:1, one launch (start us, length us, event | category | flops | bytes accessed | tf_op | source)
XLA Modules:
  0.0 442.7 jit_solution(6184211906906975168)
XLA Ops:
  7.2 16.6 %all_gather.17 = f32[1024,16]{0,1:T(8,128)} all-gather(f32[128,16]{0,1:T(8,128)} %param.36), channel_id=1, replica_groups=mesh['ctx'=8,'ch'=16] {'ctx'}, dimensions={0}, use_global_device_ids=true | all-gather | bytes 73728 | tf_op jit(solution)/shard_map/all_gather | solution.py:193
  26.8 7.5 %all-reduce.2 = s32[16]{0:T(128)S(1)} all-reduce(s32[16]{0:T(128)S(1)} %dynamic-update-slice.24), channel_id=1, replica_groups=mesh['ctx'=8,'ch'=16] {'ctx'}, use_global_device_ids=true, to_apply=%add.2 | all-reduce | flops 16 | bytes 128
  36.7 14.9 %all_gather.16 = bf16[16,64,256]{2,1,0:T(8,128)(2,1)S(1)} all-gather(bf16[2,64,256]{2,1,0:T(8,128)(2,1)S(1)} %bitcast.451), channel_id=1, replica_groups=mesh['ctx'=8,'ch'=16] {'ctx'}, dimensions={0}, use_global_device_ids=true | all-gather | bytes 589824 | tf_op jit(solution)/shard_map/all_gather | solution.py:129
  51.6 13.3 %all_gather.19 = bf16[16,64,256]{2,1,0:T(8,128)(2,1)S(1)} all-gather(bf16[2,64,256]{2,1,0:T(8,128)(2,1)S(1)} %bitcast.450), channel_id=1, replica_groups=mesh['ctx'=8,'ch'=16] {'ctx'}, dimensions={0}, use_global_device_ids=true | all-gather | bytes 589824 | tf_op jit(solution)/shard_map/all_gather | solution.py:130
  75.1 3.0 fusion.56
  78.2 3.0 fusion.58
  81.5 4.1 fusion.22
  116.0 6.0 %copy_bitcast_fusion = (f32[16,128,256]{2,1,0:T(8,128)}, f32[16,128,256]{2,1,0:T(8,128)}) fusion(f32[16,16,8,256]{3,1,2,0:T(8,128)S(1)} %subtract_bitcast_fusion.1, f32[16,16,8,256]{3,1,2,0:T(8,128)S(1)} %add_bitcast_fusion.1), kind=kLoop, calls=%fused_computation.92 | loop fusion | bytes 8388608 | tf_op jit(solution)/shard_map/reshape | solution.py:52
  122.0 5.8 %copy_bitcast_fusion.2 = (f32[16,128,256]{2,1,0:T(8,128)}, f32[16,128,256]{2,1,0:T(8,128)}) fusion(f32[16,16,8,256]{3,1,2,0:T(8,128)S(1)} %subtract_bitcast_fusion.2, f32[16,16,8,256]{3,1,2,0:T(8,128)S(1)} %add_bitcast_fusion.2), kind=kLoop, calls=%fused_computation.94 | loop fusion | bytes 8388608 | tf_op jit(solution)/shard_map/tile;reshape | solution.py:122
  127.8 5.8 %copy_bitcast_fusion.4 = (f32[16,128,256]{2,1,0:T(8,128)}, f32[16,128,256]{2,1,0:T(8,128)}) fusion(f32[16,16,8,256]{3,1,2,0:T(8,128)S(1)} %subtract_bitcast_fusion.3, f32[16,16,8,256]{3,1,2,0:T(8,128)S(1)} %add_bitcast_fusion.3), kind=kLoop, calls=%fused_computation.96 | loop fusion | bytes 8388608 | tf_op jit(solution)/shard_map/reshape | solution.py:52
  136.1 171.2 %while.31 = (s32[]{:T(128)}, f32[2,128,256]{2,1,0:T(8,128)}, f32[2,128,256]{2,1,0:T(8,128)S(1)}, f32[2,128,256]{2,1,0:T(8,128)S(1)}, f32[2,128,256]{2,1,0:T(8,12...) while((s32[]{:T(128)}, f32[2,128,256]{2,1,0:T(8,128)}, ...), condition=%wide.region_9.10_spmd, body=%wide.region_0.9_spmd.sunk | while | flops 1572892 | bytes 7865301 | solution.py:177
  143.0 3.0 conditional.8
  163.7 3.0 conditional.8
  186.4 3.0 conditional.8
  195.1 3.0 conditional.8
  249.9 3.0 conditional.8
  262.7 2.9 conditional.8
  272.5 3.0 conditional.8
  281.3 3.0 conditional.8
  316.7 3.2 subtract_bitcast_fusion
  319.8 3.0 fusion.28
  322.9 3.2 multiply_bitcast_fusion
  334.5 68.9 %reduce-scatter.3.cloned.1.call-done = f32[16,64,16]{1,0,2:T(8,128)} async-done(((f32[16,64,256]{1,0,2:T(8,128)}), f32[16,64,16]{1,0,2:T(8,128)}) %reduce-scatter.3.cloned.1.call-update) | async-done | bytes 65552 | tf_op jit(solution)/shard_map/reduce_scatter | solution.py:204
  405.7 28.8 %reduce-scatter.5.cloned.1.call-done = f32[2,64,16]{1,2,0:T(8,128)} async-done(((f32[16,64,16]{1,2,0:T(8,128)}), f32[2,64,16]{1,2,0:T(8,128)}) %reduce-scatter.5.cloned.1.call-update) | async-done | bytes 8208 | tf_op jit(solution)/shard_map/reduce_scatter | solution.py:205
  (269 shorter events, 251.1 us)
Async XLA Ops:
  7.2 29.5 %copy-start.6 = (bf16[128,256]{1,0:T(8,128)(2,1)S(1)}, bf16[128,256]{1,0:T(8,128)(2,1)}, u32[]{:S(2)}) copy-start(bf16[128,256]{1,0:T(8,128)(2,1)} %param.34) | copy-start | bytes 196612
  7.2 29.5 %copy-start.7 = (bf16[128,256]{1,0:T(8,128)(2,1)S(1)}, bf16[128,256]{1,0:T(8,128)(2,1)}, u32[]{:S(2)}) copy-start(bf16[128,256]{1,0:T(8,128)(2,1)} %param.33) | copy-start | bytes 196612
  7.2 66.1 %all-gather.2.cloned.1.call-start = ((), (), s32[]{:S(2)}) async-start(), calls=%async_computation.2 | async-start | bytes 1114112 | tf_op jit(solution)/shard_map/all_gather | solution.py:194
  23.9 379.6 %reduce-scatter.3.cloned.1.call-start = ((), (), s32[]{:S(2)}) async-start(), calls=%async_computation.3 | async-start | bytes 2228224 | tf_op jit(solution)/shard_map/reduce_scatter | solution.py:204
  64.8 6.0 %copy-start.4 = (bf16[16,64,256]{2,1,0:T(8,128)(2,1)}, bf16[16,64,256]{2,1,0:T(8,128)(2,1)S(1)}, u32[]{:S(2)}) copy-start(bf16[16,64,256]{2,1,0:T(8,128)(2,1)S(1)} %all_gather.19) | copy-start | bytes 1572868
  75.1 6.1 %copy-start.5 = (bf16[16,64,256]{2,1,0:T(8,128)(2,1)S(1)}, bf16[16,64,256]{2,1,0:T(8,128)(2,1)}, u32[]{:S(2)}) copy-start(bf16[16,64,256]{2,1,0:T(8,128)(2,1)} %copy-done.4) | copy-start | bytes 1572868
  78.2 3.1 copy-start.2
  78.2 3.1 copy-start.3
  134.4 1.7 copy-start.9
  309.7 2.5 copy-start.1
  312.2 1.8 copy-start
  329.5 105.0 %reduce-scatter.5.cloned.1.call-start = ((), (), s32[]{:S(2)}) async-start(), calls=%async_computation.4 | async-start | bytes 147456 | tf_op jit(solution)/shard_map/reduce_scatter | solution.py:205
  331.7 73.4 %copy-start.8 = (bf16[128,256]{1,0:T(8,128)(2,1)S(1)}, bf16[128,256]{1,0:T(8,128)(2,1)}, u32[]{:S(2)}) copy-start(bf16[128,256]{1,0:T(8,128)(2,1)} %param.35) | copy-start | bytes 196612
Sparse Core Ops, SparseCore 0:
  24.0 41.8 all-gather.1
  329.6 73.7 reduce-scatter.2
  405.9 28.5 reduce-scatter.4
where the time goes:
time: 450 us; the launch traced here: 443 us
  local copies, waits for them, and re-layouts  102 us (23%)
  waiting for transfers between devices  97.8 us (22%)
  matrix products  71.6 us (16%)
  other arithmetic  59.5 us (13%)
  blocking collectives  52.3 us (12%)
  loops' own time  43.6 us (10%)
  between operations  15.4 us (3%)
    reduce_scatter x1, waiting for transfers between devices, local(): lax.psum_scatter(per_filter, 'ch', scatter_dimension=2, tiled=True)  68.9 us
    dynamic_update_slice x22, other arithmetic, ahead_terms(): s_im = lax.dynamic_update_index_in_dim(s_im, old_im + cross_im, level, 0)  44 us
    another operation x1, loops' own time, pair_sums(): totals = lax.fori_loop(0, piece_ids.shape[0], one_block, start_carry)  42.5 us
    reduce_scatter x1, waiting for transfers between devices, local(): lax.psum_scatter(partial_sum, 'ctx', scatter_dimension=0, tiled=True)  28.8 us
    dynamic_slice x22, local copies, waits for them, and re-layouts, ahead_terms(): old_re = lax.dynamic_index_in_dim(s_re, level, 0, keepdims=False)  20.4 us
    all_gather x1, blocking collectives, local(): lag_cols = lax.all_gather(filters, 'ctx', axis=0, tiled=True)  16.6 us
    squeeze x16, local copies, waits for them, and re-layouts, one_block(): g_im = lax.dynamic_index_in_dim(pg_im, index, 0, keepdims=False)  15.9 us
    squeeze x16, local copies, waits for them, and re-layouts, one_block(): u_im = lax.dynamic_index_in_dim(pu_im, index, 0, keepdims=False)  15.9 us
  transfers between devices with their start and end apart: 3, of which 2 were waited for; matrix products, arithmetic and copies ran while one was open for 4% of the time, Pallas kernels for 0%

commit v1 on v0

v1 whole, which is shorter than its diff:
```python
from functools import partial

import jax
import jax.numpy as jnp
from jax import lax
from jax.experimental import pallas as pl
from jax.experimental.pallas import tpu as pltpu
from jax.sharding import PartitionSpec as P

MESH = pl.DeviceIdType.MESH
BF16 = jnp.bfloat16
F32 = jnp.float32
HALF = 64
SPAN = 128


def iota(shape, dim):
    return lax.broadcasted_iota(jnp.int32, shape, dim)


def mm(left, right, dims=((1,), (0,))):
    return lax.dot_general(left, right, (dims, ((), ())), preferred_element_type=F32)


def wait_all(ref, count, sem):
    view = ref.at[pl.ds(0, count)]
    pltpu.make_async_copy(view, view, sem).wait()


def swap_matrix(outer, inner):
    size = outer * inner
    row = iota((size, size), 0)
    col = iota((size, size), 1)
    hit = (row // outer == col % inner) & (row % outer == col // inner)
    return jnp.where(hit, 1.0, 0.0).astype(BF16)


def toeplitz(taps, length):
    base = jnp.broadcast_to(taps, (8, length))
    row = iota((8, length), 0)
    for bit in (1, 2, 4):
        base = jnp.where((row & bit) != 0, pltpu.roll(base, bit, 1), base)
    rows = [base] + [pltpu.roll(base, 8 * k, 1) for k in range(1, SPAN // 8)]
    full = jnp.concatenate(rows, axis=0)
    keep = iota((SPAN, length), 1) >= iota((SPAN, length), 0)
    return jnp.where(keep, full, 0.0)


def diagonals(table, length):
    keep = iota((SPAN, length), 1) >= iota((SPAN, length), 0)
    table = jnp.where(keep, table, 0.0)
    total = table[:8]
    for k in range(1, SPAN // 8):
        total = total + pltpu.roll(table[8 * k : 8 * k + 8], length - 8 * k, 1)
    row = iota((8, length), 0)
    for bit in (1, 2, 4):
        total = jnp.where((row & bit) != 0, pltpu.roll(total, length - bit, 1), total)
    return jnp.sum(total, axis=0, keepdims=True)


def kernel(
    nz,
    nj,
    nf,
    ids_ref,
    og_ref,
    ig_ref,
    sg_ref,
    ct_ref,
    fl_ref,
    outer_ref,
    inner_ref,
    signal_ref,
    fgrad_ref,
    w_send,
    w_recv,
    b_send,
    b_recv,
    a_send,
    a_recv,
    a2_send,
    a2_recv,
    b2_send,
    b2_recv,
    g_send,
    g_recv,
    send_sems,
    recv_sems,
):
    zi = lax.axis_index("ctx")
    ji = lax.axis_index("ch")
    nr = nf // nz
    rows = nz * nj
    length = nz * SPAN

    def ctx_peer(step):
        return lax.rem(zi + step, nz)

    def ch_peer(step):
        return lax.rem(ji + step, nj)

    barrier = pltpu.get_barrier_semaphore()
    for step in range(1, nz):
        pl.semaphore_signal(barrier, inc=1, device_id=(ctx_peer(step), ji), device_id_type=MESH)
    for step in range(1, nj):
        pl.semaphore_signal(barrier, inc=1, device_id=(zi, ch_peer(step)), device_id_type=MESH)

    def over_ctx(send, recv, k):
        for step in range(1, nz):
            q = ctx_peer(step)
            pltpu.make_async_remote_copy(
                send.at[q], recv.at[zi], send_sems.at[k], recv_sems.at[k], (q, ji), MESH
            ).start()
        recv[zi] = send[zi]

    def over_ch(send, recv, k):
        for step in range(1, nj):
            j = ch_peer(step)
            pltpu.make_async_remote_copy(
                send.at[j], recv.at[ji], send_sems.at[k], recv_sems.at[k], (zi, j), MESH
            ).start()
        recv[ji] = send[ji]

    product = ig_ref[...].astype(F32) * sg_ref[...].astype(F32)
    weighted = ct_ref[...].astype(F32) * og_ref[...].astype(F32)
    b_send[:, 0] = product.T.astype(BF16).reshape(nj, nf, SPAN)
    b_send[:, 1] = weighted.T.astype(BF16).reshape(nj, nf, SPAN)

    taps = fl_ref[...].T
    row8 = iota((8, SPAN), 0)
    id_lo = ids_ref[0].astype(F32)
    id_hi = ids_ref[1].astype(F32)
    tail = jnp.where(row8 == nr, id_lo, jnp.where(row8 == nr + 1, id_hi, 0.0))
    for q in range(nz):
        w_send[q] = tail
        w_send[q, 0:nr] = taps[q * nr : (q + 1) * nr]

    pl.semaphore_wait(barrier, nz + nj - 2)
    over_ch(b_send, b_recv, 0)
    over_ctx(w_send, w_recv, 1)

    swap = swap_matrix(nj, nf)
    wait_all(w_recv, nz - 1, recv_sems.at[1])
    bands = []
    for r in range(nr):
        line = jnp.concatenate([w_recv[z, r : r + 1] for z in range(nz)], axis=1)
        bands.append(toeplitz(line, length).astype(BF16))
    row = iota((rows, rows), 0)
    col = iota((rows, rows), 1)
    same_c = (row % nj) == (col % nj)
    by_row, by_col = [], []
    for h in range(2):
        lines = [w_recv[z, nr + h : nr + h + 1] for z in range(nz)]
        by_row.append(
            jnp.concatenate([jnp.broadcast_to(v[:, :rows], (nj, rows)) for v in lines], axis=0)
        )
        lane = iota((1, rows), 1) // nj
        mixed = jnp.zeros((1, rows), F32)
        for z in range(nz):
            mixed = jnp.where(lane == z, lines[z][:, :rows], mixed)
        by_col.append(jnp.broadcast_to(mixed, (rows, rows)))

    def one_hot(hit):
        return jnp.where(hit & same_c, 1.0, 0.0).astype(BF16)

    to_pos, to_store = [], []
    for kind in range(2):
        to_pos.append(
            [one_hot(by_col[h] == (2 * (row // nj) + (h ^ kind)).astype(F32)) for h in range(2)]
        )
        to_store.append(
            [one_hot(by_row[h ^ kind] == (2 * (col // nj) + h).astype(F32)) for h in range(2)]
        )

    def stack(parts):
        return jnp.concatenate([jnp.concatenate(part, axis=1) for part in parts], axis=0)

    to_pos = stack(to_pos)
    to_store = stack(to_store)

    def reorder(matrix, values):
        low = (iota(values.shape, 1) % SPAN) < HALF
        zero = jnp.zeros_like(values)
        halves = jnp.concatenate(
            [jnp.where(low, values, zero), jnp.where(low, zero, values)], axis=0
        )
        moved = mm(matrix, halves)
        parts = []
        for k in range(values.shape[1] // SPAN):
            lanes = slice(k * SPAN, (k + 1) * SPAN)
            parts.append(moved[:rows, lanes] + pltpu.roll(moved[rows:, lanes], HALF, 1))
        return parts

    wait_all(b_recv, nj - 1, recv_sems.at[0])
    arrived = jnp.concatenate(
        [b_recv[:, k].reshape(nj * nf, SPAN) for k in range(2)], axis=1
    )
    turned = mm(swap, arrived).astype(BF16)
    for k in range(2):
        a_send[:, k] = turned[:, k * SPAN : (k + 1) * SPAN].reshape(nz, nr, nj, SPAN)
    over_ctx(a_send, a_recv, 2)
    wait_all(a_recv, nz - 1, recv_sems.at[2])
    stored = jnp.concatenate(
        [a_recv[:, k, r].reshape(rows, SPAN) for k in range(2) for r in range(nr)], axis=1
    )
    ordered = reorder(to_pos, stored)

    results = [None] * (2 * nr)
    for r in range(nr):
        p = ordered[r].astype(BF16)
        g = ordered[nr + r].astype(BF16)
        band = bands[r]
        ahead = mm(p, band)
        stacked = jnp.concatenate(
            [band[:, d * SPAN : (d + 1) * SPAN] for d in range(nz)], axis=0
        )
        behind = mm(g, stacked, ((1,), (1,)))
        conv, back = [], []
        for t in range(nz):
            conv.append(
                sum(
                    ahead[i * nj : (i + 1) * nj, (t - i) * SPAN : (t - i + 1) * SPAN]
                    for i in range(t + 1)
                )
            )
            back.append(
                sum(
                    behind[j * nj : (j + 1) * nj, (j - t) * SPAN : (j - t + 1) * SPAN]
                    for j in range(t, nz)
                )
            )
        results[r] = jnp.concatenate(conv, axis=0).astype(BF16)
        results[nr + r] = jnp.concatenate(back, axis=0).astype(BF16)

    restored = reorder(to_store, jnp.concatenate(results, axis=1))
    for k in range(2):
        for r in range(nr):
            a2_send[:, k, r] = restored[k * nr + r].astype(BF16).reshape(nz, nj, SPAN)
    over_ctx(a2_send, a2_recv, 3)

    sums = []
    for r in range(nr):
        p_turned = ordered[r].T.astype(BF16)
        g = ordered[nr + r].astype(BF16)
        shifted = [g] + [
            jnp.concatenate([g[d * nj :], jnp.zeros((d * nj, SPAN), BF16)], axis=0)
            for d in range(1, nz)
        ]
        sums.append(diagonals(mm(p_turned, jnp.concatenate(shifted, axis=1)), length))
    for z in range(nz):
        tile = jnp.zeros((8, SPAN), F32)
        for r in range(nr):
            tile = jnp.where(row8 == r, sums[r][:, z * SPAN : (z + 1) * SPAN], tile)
        g_send[z] = tile
    over_ctx(g_send, g_recv, 4)

    wait_all(a2_recv, nz - 1, recv_sems.at[3])
    came = jnp.concatenate(
        [a2_recv[:, k].reshape(nf * nj, SPAN) for k in range(2)], axis=1
    )
    back_turned = mm(swap.T if nj != nf else swap, came).astype(BF16)
    for k in range(2):
        b2_send[:, k] = back_turned[:, k * SPAN : (k + 1) * SPAN].reshape(nj, nf, SPAN)
    over_ch(b2_send, b2_recv, 5)

    wait_all(g_recv, nz - 1, recv_sems.at[4])
    grads = jnp.concatenate([g_recv[q, 0:nr] for q in range(nz)], axis=0)
    fgrad_ref[...] = grads.T

    wait_all(b2_recv, nj - 1, recv_sems.at[5])
    conv = b2_recv[:, 0].reshape(nj * nf, SPAN).astype(F32).T
    back = b2_recv[:, 1].reshape(nj * nf, SPAN).astype(F32).T
    outer_ref[...] = (ct_ref[...].astype(F32) * conv).astype(BF16)
    inner_ref[...] = (back * sg_ref[...].astype(F32)).astype(BF16)
    signal_ref[...] = (back * ig_ref[...].astype(F32)).astype(BF16)

    for k, (send, count) in enumerate(
        ((b_send, nj), (w_send, nz), (a_send, nz), (a2_send, nz), (g_send, nz), (b2_send, nj))
    ):
        wait_all(send, count - 1, send_sems.at[k])


def solution(mesh):
    nz = mesh.shape["ctx"]
    nj = mesh.shape["ch"]

    def local(out_gate, in_gate, signal, cotangent, filters, block_ids):
        tokens, width = out_gate.shape
        nf = filters.shape[1]
        nr = nf // nz
        vmem = pl.BlockSpec(memory_space=pltpu.VMEM)
        grad = jax.ShapeDtypeStruct((tokens, width), BF16)
        lag = pltpu.VMEM((nz, 8, SPAN), F32)
        by_ch = pltpu.VMEM((nj, 2, nf, SPAN), BF16)
        by_ctx = pltpu.VMEM((nz, 2, nr, nj, SPAN), BF16)
        return pl.pallas_call(
            partial(kernel, nz, nj, nf),
            out_shape=(grad, grad, grad, jax.ShapeDtypeStruct(filters.shape, F32)),
            in_specs=[pl.BlockSpec(memory_space=pltpu.SMEM)] + [vmem] * 5,
            out_specs=(vmem,) * 4,
            scratch_shapes=[
                lag,
                lag,
                by_ch,
                by_ch,
                by_ctx,
                by_ctx,
                by_ctx,
                by_ctx,
                by_ch,
                by_ch,
                lag,
                lag,
                pltpu.SemaphoreType.DMA((6,)),
                pltpu.SemaphoreType.DMA((6,)),
            ],
            compiler_params=pltpu.CompilerParams(
                collective_id=0, has_side_effects=True, vmem_limit_bytes=48 * 1024 * 1024
            ),
        )(block_ids, out_gate, in_gate, signal, cotangent, filters)

    return jax.shard_map(
        local,
        mesh=mesh,
        in_specs=(P("ctx", "ch"),) * 5 + (P("ctx"),),
        out_specs=(P("ctx", "ch"),) * 4,
        check_vma=False,
    )
```

time: 450 us -> 35.6 us (0.08); the launches traced: 443 us -> 35.3 us
  waiting for transfers between devices: 97.8 us -> 0 us
  local copies, waits for them, and re-layouts: 102 us -> 5.91 us
  matrix products: 71.6 us -> 0 us
  other arithmetic: 59.5 us -> 0 us
  blocking collectives: 52.3 us -> 0 us
  loops' own time: 43.6 us -> 0 us
  Pallas kernels: 0 us -> 28.8 us
  between operations: 15.4 us -> 0.68 us
    reduce_scatter x2 -> x0, waiting for transfers between devices: 97.8 us -> none  [the longest x1 68.9 us: local(): lax.psum_scatter(per_filter, 'ch', scatter_dimension=2, tiled=True)]
    dot_general x42 -> x0, matrix products: 71.6 us -> none  [the longest x4 9.93 us: forward(): a_re = jnp.einsum(section_one, cos_one, shaped, precision=exact_mode)]
    all_gather x3 -> x0, blocking collectives: 44.8 us -> none  [the longest x1 16.6 us: local(): lag_cols = lax.all_gather(filters, 'ctx', axis=0, tiled=True)]
    dynamic_update_slice x22 -> x0, other arithmetic: 44 us -> none  [ahead_terms(): s_im = lax.dynamic_update_index_in_dim(s_im, old_im + cross_im, level, 0)]
    another operation x65 -> x0, loops' own time: 43.6 us -> none  [the longest x1 42.5 us: pair_sums(): totals = lax.fori_loop(0, piece_ids.shape[0], one_block, start_carry)]
    squeeze x32 -> x0, local copies, waits for them, and re-layouts: 31.8 us -> none  [the longest x16 15.9 us: one_block(): g_im = lax.dynamic_index_in_dim(pg_im, index, 0, keepdims=False)]
    dynamic_slice x38 -> x0, local copies, waits for them, and re-layouts: 29.7 us -> none  [the longest x22 20.4 us: ahead_terms(): old_re = lax.dynamic_index_in_dim(s_re, level, 0, keepdims=False)]
    pallas_call x0 -> x1, Pallas kernels: none -> 28.8 us  [local(): pl.pallas_call(partial(kernel, nz, nj, nf), out_shape=(grad, grad, grad,...]
  transfers between devices with their start and end apart: 3 -> 0, of which waited for: 2 -> 0; matrix products, arithmetic and copies ran while one was open for 4% -> 0% of each run, Pallas kernels for 0% -> 0%
where the time goes in v1:
time: 35.6 us; the launch traced here: 35.3 us
  Pallas kernels  28.8 us (81%)
  local copies, waits for them, and re-layouts  5.91 us (17%)
  between operations  0.68 us (2%)
    pallas_call x1, Pallas kernels, local(): pl.pallas_call(partial(kernel, nz, nj, nf), out_shape=(grad, grad, grad,...  28.8 us
    unnamed x14, local copies, waits for them, and re-layouts  5.24 us

profile of v1, /device:TPU:1, one launch (start us, length us, event | category | flops | bytes accessed | tf_op | source)
XLA Modules:
  0.0 35.3 jit_solution(770925596710791006)
XLA Ops:
  0.6 0.0 copy-start.4
  0.6 0.0 copy-start
  0.7 0.8 %copy.10.fl_ref = f32[128,16]{1,0:T(8,128)S(1)} copy(f32[128,16]{0,1:T(8,128)} %param.10) | data formatting | bytes 16384 | tf_op args[4]
  1.5 0.0 copy-done.4
  1.5 0.0 copy-done
  1.5 0.0 copy-start.1
  1.5 0.8 %copy-done.1 = bf16[128,256]{1,0:T(8,128)(2,1)S(1)} copy-done((bf16[128,256]{1,0:T(8,128)(2,1)S(1)}, bf16[128,256]{1,0:T(8,128)(2,1)}, u32[]{:S(2)}) %copy-start.1) | copy-done | bytes 65560
  2.3 0.0 copy-start.2
  2.3 0.8 %copy-done.2 = bf16[128,256]{1,0:T(8,128)(2,1)S(1)} copy-done((bf16[128,256]{1,0:T(8,128)(2,1)S(1)}, bf16[128,256]{1,0:T(8,128)(2,1)}, u32[]{:S(2)}) %copy-start.2) | copy-done | bytes 65560
  3.2 0.0 copy-start.3
  3.2 0.8 %copy-done.3 = bf16[128,256]{1,0:T(8,128)(2,1)S(1)} copy-done((bf16[128,256]{1,0:T(8,128)(2,1)S(1)}, bf16[128,256]{1,0:T(8,128)(2,1)}, u32[]{:S(2)}) %copy-start.3) | copy-done | bytes 65560
  4.0 28.8 %shard_map.93 = (bf16[128,256]{1,0:T(8,128)(2,1)S(1)}, bf16[128,256]{1,0:T(8,128)(2,1)S(1)}, bf16[128,256]{1,0:T(8,128)(2,1)S(1)}, f32[128,16]{1,0:T(8,128)S(1)}) custom-call(s32[2]{0:T(128)S(1)} %copy-done.4, bf16[128,256]{1,0:T(8,128)(2,1)S(1)} %copy-done, bf16[128,256]{1,0:T(8,128)(2,1)S(1)} %copy-done.1, bf16[128,256]{1,0:T(8,128)(2,1)S(1)} %copy-done.2, ...), custom_call_target="tpu_custom_call" | custom-call | tf_op jit(solution)/shard_map/pallas_call | solution.py:296
  32.8 0.7 %copy.11 = f32[128,16]{0,1:T(8,128)} copy(f32[128,16]{1,0:T(8,128)S(1)} %get-tuple-element.7) | data formatting | bytes 16384 | tf_op jit(solution)/shard_map/pallas_call | solution.py:296
  33.4 0.6 %copy.15 = bf16[128,256]{1,0:T(8,128)(2,1)} copy(bf16[128,256]{1,0:T(8,128)(2,1)S(1)} %get-tuple-element.12) | data formatting | bytes 131072
  34.1 0.6 %copy.16 = bf16[128,256]{1,0:T(8,128)(2,1)} copy(bf16[128,256]{1,0:T(8,128)(2,1)S(1)} %get-tuple-element.13) | data formatting | bytes 131072
  34.7 0.6 %copy.17 = bf16[128,256]{1,0:T(8,128)(2,1)} copy(bf16[128,256]{1,0:T(8,128)(2,1)S(1)} %get-tuple-element.14) | data formatting | bytes 131072
Async XLA Ops:
  0.6 0.9 %copy-start.4 = (s32[2]{0:T(128)S(1)}, s32[2]{0:T(128)}, u32[]{:S(2)}) copy-start(s32[2]{0:T(128)} %ids_ref.1) | copy-start | bytes 28
  0.6 0.8 %copy-start = (bf16[128,256]{1,0:T(8,128)(2,1)S(1)}, bf16[128,256]{1,0:T(8,128)(2,1)}, u32[]{:S(2)}) copy-start(bf16[128,256]{1,0:T(8,128)(2,1)} %og_ref.1) | copy-start | bytes 196612
  1.5 0.8 %copy-start.1 = (bf16[128,256]{1,0:T(8,128)(2,1)S(1)}, bf16[128,256]{1,0:T(8,128)(2,1)}, u32[]{:S(2)}) copy-start(bf16[128,256]{1,0:T(8,128)(2,1)} %ig_ref.1) | copy-start | bytes 196612
  2.3 0.8 %copy-start.2 = (bf16[128,256]{1,0:T(8,128)(2,1)S(1)}, bf16[128,256]{1,0:T(8,128)(2,1)}, u32[]{:S(2)}) copy-start(bf16[128,256]{1,0:T(8,128)(2,1)} %sg_ref.1) | copy-start | bytes 196612
  3.2 0.8 %copy-start.3 = (bf16[128,256]{1,0:T(8,128)(2,1)S(1)}, bf16[128,256]{1,0:T(8,128)(2,1)}, u32[]{:S(2)}) copy-start(bf16[128,256]{1,0:T(8,128)(2,1)} %ct_ref.1) | copy-start | bytes 196612

commit v2 on v1

v2 whole, which is shorter than its diff:
```python
from functools import partial

import jax
import jax.numpy as jnp
import numpy as np
from jax import lax
from jax.experimental import pallas as pl
from jax.experimental.pallas import tpu as pltpu
from jax.sharding import PartitionSpec as P

MESH = pl.DeviceIdType.MESH
BF16 = jnp.bfloat16
F32 = jnp.float32
HALF = 64
SPAN = 128
FREQ = 128


def iota(shape, dim):
    return lax.broadcasted_iota(jnp.int32, shape, dim)


def dft_table():
    angle = np.pi * np.outer(np.arange(SPAN), 2 * np.arange(FREQ) + 1) / (2 * SPAN)
    full = np.concatenate([np.cos(angle), -np.sin(angle)], axis=1)
    high = full.astype(BF16)
    low = (full - high.astype(np.float64)).astype(BF16)
    return np.concatenate([high, low], axis=0)


def mm(left, right):
    return jnp.dot(left, right, preferred_element_type=F32)


def mm_nt(left, right):
    return lax.dot_general(left, right, (((1,), (1,)), ((), ())), preferred_element_type=F32)


def wait_bytes(ref, start, count, sem):
    view = ref.at[pl.ds(start, count)]
    pltpu.make_async_copy(view, view, sem).wait()


def split(values):
    high = values.astype(BF16)
    return high, (values - high.astype(F32)).astype(BF16)


def exchange_kernel(
    nz,
    nj,
    nf,
    ids_hbm,
    og_hbm,
    ig_hbm,
    sg_hbm,
    ct_hbm,
    fl_hbm,
    dft_hbm,
    conv_ref,
    back_ref,
    fgrad_ref,
    ig_ref,
    sg_ref,
    ct_ref,
    og_ref,
    dft_ref,
    ids_ref,
    ids_all,
    f_send,
    f_recv,
    a_send,
    a_recv,
    r_send,
    r_recv,
    g_send,
    g_recv,
    halves,
    spec,
    wspec,
    load_sems,
    send_sems,
    recv_sems,
):
    nc = 2 * nf
    nx = nj // 4
    zi = lax.axis_index("ctx")
    ji = lax.axis_index("ch")
    depth, core = zi // 2, zi % 2
    xi, yi = ji // 4, ji % 4

    def chunk_of(q):
        return 2 * lax.rem(xi + q // 2 + nx // 2, nx) + lax.rem(q + yi // 2, 2)

    def user_of(j):
        z = lax.rem(xi + nx - j // 4 + nx // 2, nx)
        return 2 * z + lax.rem(yi // 2 + j % 4 // 2, 2)

    mine = chunk_of(zi)

    loads = [
        pltpu.make_async_copy(src, dst, load_sems.at[k])
        for k, (src, dst) in enumerate(
            (
                (fl_hbm, f_send),
                (ig_hbm, ig_ref),
                (sg_hbm, sg_ref),
                (ct_hbm, ct_ref),
                (og_hbm, og_ref),
                (dft_hbm, dft_ref),
                (ids_hbm, ids_ref),
            )
        )
    ]
    for load in loads:
        load.start()

    barrier = pltpu.get_barrier_semaphore()

    def greet(device):
        pl.semaphore_signal(barrier, inc=1, device_id=device, device_id_type=MESH)

    owners = [(lax.rem(zi + s, nz), 2 * mine + r) for s in range(nz) for r in range(2)]
    users = []
    for s in range(nj):
        j = lax.rem(ji + s, nj)
        users.append((user_of(j), j))
    group = [lax.rem(zi + s, nz) for s in range(1, nz)]
    own = user_of(ji) == zi
    own_side = [2 * mine + r == ji for r in range(2)]

    for r in range(2):
        pl.when(jnp.logical_not(own_side[r]))(partial(greet, owners[r]))
    for device in owners[2:]:
        greet(device)
    for q in group:
        greet((q, ji))
    pl.when(jnp.logical_not(own))(partial(greet, users[0]))
    for device in users[1:]:
        greet(device)

    loads[0].wait()
    loads[1].wait()
    loads[2].wait()
    product = ig_ref[...].astype(F32) * sg_ref[...].astype(F32)
    a_send[:, 0] = product.T.astype(BF16).reshape(nz, nc, SPAN)
    loads[3].wait()
    loads[4].wait()
    weighted = ct_ref[...].astype(F32) * og_ref[...].astype(F32)
    a_send[:, 1] = weighted.T.astype(BF16).reshape(nz, nc, SPAN)

    pl.semaphore_wait(barrier, nz - 1 + 2 * nj - jnp.where(own, 2, 0))

    def remote(src, dst, k, device):
        return pltpu.make_async_remote_copy(
            src, dst, send_sems.at[k], recv_sems.at[k], device, MESH
        )

    f_slot = f_recv.at[zi, yi % 2]

    @pl.when(own)
    def _():
        pltpu.make_async_copy(f_send, f_slot, recv_sems.at[0]).start()

    @pl.when(jnp.logical_not(own))
    def _():
        remote(f_send, f_slot, 0, users[0]).start()

    for device in users[1:]:
        remote(f_send, f_slot, 0, device).start()

    loads[6].wait()
    for q in group:
        remote(ids_ref, ids_all.at[zi], 1, (q, ji)).start()
        remote(a_send.at[chunk_of(q)], a_recv.at[zi], 2, (q, ji)).start()
    ids_all[zi, 0] = ids_ref[0]
    ids_all[zi, 1] = ids_ref[1]
    a_recv[zi] = a_send[mine]

    wait_bytes(ids_all, 0, nz - 1, recv_sems.at[1])
    ids = [ids_all[s // 2, s % 2] for s in range(2 * nz)]
    order = []
    for n in range(2 * nz):
        place = jnp.int32(0)
        for s in range(2 * nz):
            place = jnp.where(ids[s] == n, s, place)
        order.append(place)

    loads[5].wait()
    table = dft_ref[...]
    low = iota((2 * nc, SPAN), 1) < HALF
    odd = iota((nc, FREQ), 1) % 2 == 1
    sign = jnp.where(odd, -1.0, 1.0)

    def spread(slot, values):
        turned = pltpu.roll(values, HALF, 1)
        halves[2 * slot] = jnp.where(low, values, turned)
        halves[2 * slot + 1] = jnp.where(low, turned, values)

    def pick(first, second):
        return jnp.where(low, halves[first], halves[second])

    wait_bytes(a_recv, 0, nz - 1, recv_sems.at[2])
    for z in range(nz):
        spread(z, a_recv[z].reshape(2 * nc, SPAN).astype(F32))
    blocks = [pick(order[2 * i], order[2 * i + 1]).astype(BF16) for i in range(nz)]
    blocks = jnp.concatenate(blocks, axis=0)
    spec[...] = mm(jnp.concatenate([blocks, blocks], axis=1), table).reshape(
        nz, 2, nc, 2 * FREQ
    )

    def part(ref, *at):
        value = ref[at]
        return value[:, :FREQ], value[:, FREQ:]

    def times(total, left, right):
        (a, b), (c, d) = left, right
        re, im = a * c - b * d, a * d + b * c
        return (re, im) if total is None else (total[0] + re, total[1] + im)

    def against(total, left, right):
        (a, b), (c, d) = left, right
        re, im = a * c + b * d, a * d - b * c
        return (re, im) if total is None else (total[0] + re, total[1] + im)

    cross = [None] * (nz + 1)
    for d in range(nz):
        for i in range(nz - d):
            cross[d] = against(cross[d], part(spec, i, 0), part(spec, i + d, 1))
    rows = []
    for d in range(nz):
        re, im = cross[d]
        if d + 1 < nz:
            re = re + sign * cross[d + 1][1]
            im = im - sign * cross[d + 1][0]
        rows.append(jnp.concatenate([re, im], axis=1))
    high, rest = split(jnp.concatenate(rows, axis=0))
    lags = mm_nt(high, table)
    lags = lags[:, :SPAN] + lags[:, SPAN:] + mm_nt(rest, table[:SPAN])
    g_send[...] = (lags * (1.0 / SPAN)).reshape(nz, 2, nf, SPAN)

    g_slot = g_recv.at[ji]
    for r in range(2):
        src = g_send.at[zi, r]

        def keep(src=src):
            pltpu.make_async_copy(src, g_slot, recv_sems.at[3]).start()

        def pass_on(src=src, r=r):
            remote(src, g_slot, 3, owners[r]).start()

        pl.when(own_side[r])(keep)
        pl.when(jnp.logical_not(own_side[r]))(pass_on)
    for s in range(1, nz):
        for r in range(2):
            z, j = owners[2 * s + r]
            remote(g_send.at[z, r], g_slot, 3, (z, j)).start()

    wait_bytes(f_recv, 0, nz, recv_sems.at[0])
    high, rest = split(f_recv[...].reshape(nz * nc, SPAN))
    raw = mm(jnp.concatenate([high, high], axis=1), table) + mm(rest, table[:SPAN])
    raw = raw.reshape(nz, nc, 2 * FREQ)
    for d in range(nz):
        re, im = raw[d, :, :FREQ], raw[d, :, FREQ:]
        if d:
            re = re - sign * raw[d - 1, :, FREQ:]
            im = im + sign * raw[d - 1, :, :FREQ]
        wspec[d, :, :FREQ] = re
        wspec[d, :, FREQ:] = im

    rows = []
    for m in range(nz):
        conv = back = None
        for i in range(m + 1):
            conv = times(conv, part(wspec, m - i), part(spec, i, 0))
        for j in range(m, nz):
            back = against(back, part(wspec, j - m), part(spec, j, 1))
        rows += [jnp.concatenate(conv, axis=1), jnp.concatenate(back, axis=1)]
    result = mm_nt(jnp.concatenate(rows, axis=0).astype(BF16), table)
    result = (result[:, :SPAN] + result[:, SPAN:]) * (1.0 / SPAN)
    for i in range(nz):
        spread(i, result[2 * nc * i : 2 * nc * (i + 1)])
    for z in range(nz):
        r_send[z] = pick(ids[2 * z], ids[2 * z + 1]).astype(BF16).reshape(2, nc, SPAN)
    for q in group:
        remote(r_send.at[q], r_recv.at[mine], 4, (q, ji)).start()
    r_recv[mine] = r_send[zi]

    wait_bytes(g_recv, 0, nj, recv_sems.at[3])
    total = g_recv[0]
    for j in range(1, nj):
        total = total + g_recv[j]
    fgrad_ref[...] = total

    wait_bytes(r_recv, 0, nz - 1, recv_sems.at[4])
    conv_ref[...] = r_recv[:, 0].reshape(nz * nc, SPAN)
    back_ref[...] = r_recv[:, 1].reshape(nz * nc, SPAN)

    wait_bytes(ids_all, 0, nz - 1, send_sems.at[1])
    wait_bytes(a_send, 0, nz - 1, send_sems.at[2])
    wait_bytes(r_send, 0, nz - 1, send_sems.at[4])

    @pl.when(own)
    def _():
        wait_bytes(g_recv, 0, nj - 1, send_sems.at[0])
        wait_bytes(g_recv, 0, nj - 1, send_sems.at[3])

    @pl.when(jnp.logical_not(own))
    def _():
        wait_bytes(g_recv, 0, nj, send_sems.at[0])
        wait_bytes(g_recv, 0, nj, send_sems.at[3])


def gate_kernel(
    conv_ref,
    back_ref,
    fgrad_ref,
    ig_ref,
    sg_ref,
    ct_ref,
    outer_hbm,
    inner_hbm,
    signal_hbm,
    fgrad_hbm,
    outer,
    inner,
    signal,
    sems,
):
    def put(src, dst, k):
        copy = pltpu.make_async_copy(src, dst, sems.at[k])
        copy.start()
        return copy

    copies = [put(fgrad_ref, fgrad_hbm, 0)]
    conv = conv_ref[...].astype(F32).T
    outer[...] = (ct_ref[...].astype(F32) * conv).astype(BF16)
    copies.append(put(outer, outer_hbm, 1))
    back = back_ref[...].astype(F32).T
    inner[...] = (back * sg_ref[...].astype(F32)).astype(BF16)
    copies.append(put(inner, inner_hbm, 2))
    signal[...] = (back * ig_ref[...].astype(F32)).astype(BF16)
    copies.append(put(signal, signal_hbm, 3))
    for copy in copies:
        copy.wait()


def solution(mesh):
    nz = mesh.shape["ctx"]
    nj = mesh.shape["ch"]

    def local(out_gate, in_gate, signal, cotangent, filters, block_ids):
        tokens, width = out_gate.shape
        nf = filters.shape[1]
        nc = 2 * nf
        vmem = pl.BlockSpec(memory_space=pltpu.VMEM)
        anywhere = pl.BlockSpec(memory_space=pltpu.HBM)
        grad = jax.ShapeDtypeStruct((tokens, width), BF16)
        turned = jax.ShapeDtypeStruct((width, tokens), BF16)
        tokens_vmem = pltpu.VMEM((tokens, width), BF16)
        block = pltpu.VMEM((nz, 2, nc, SPAN), BF16)
        held = pl.pallas_call(
            partial(exchange_kernel, nz, nj, nf),
            out_shape=(turned, turned, jax.ShapeDtypeStruct((nf, SPAN), F32), grad, grad, grad),
            in_specs=[anywhere] * 7,
            out_specs=(vmem,) * 6,
            scratch_shapes=[
                tokens_vmem,
                pltpu.VMEM((2 * SPAN, 2 * FREQ), BF16),
                pltpu.SMEM((2,), jnp.int32),
                pltpu.SMEM((nz, 2), jnp.int32),
                pltpu.VMEM((nf, SPAN), F32),
                pltpu.VMEM((nz, 2, nf, SPAN), F32),
                block,
                block,
                block,
                block,
                pltpu.VMEM((nz, 2, nf, SPAN), F32),
                pltpu.VMEM((nj, nf, SPAN), F32),
                pltpu.VMEM((2 * nz, 2 * nc, SPAN), F32),
                pltpu.VMEM((nz, 2, nc, 2 * FREQ), F32),
                pltpu.VMEM((nz, nc, 2 * FREQ), F32),
                pltpu.SemaphoreType.DMA((7,)),
                pltpu.SemaphoreType.DMA((5,)),
                pltpu.SemaphoreType.DMA((5,)),
            ],
            compiler_params=pltpu.CompilerParams(
                collective_id=0, has_side_effects=True, vmem_limit_bytes=48 * 1024 * 1024
            ),
        )(
            *(
                pltpu.with_memory_space_constraint(value, pltpu.HBM)
                for value in (
                    block_ids,
                    out_gate,
                    in_gate,
                    signal,
                    cotangent,
                    filters.T,
                    jnp.asarray(dft_table()),
                )
            ),
        )
        *grads, fgrad = pl.pallas_call(
            gate_kernel,
            out_shape=(grad, grad, grad, jax.ShapeDtypeStruct((nf, SPAN), F32)),
            in_specs=[vmem] * 6,
            out_specs=(anywhere,) * 4,
            scratch_shapes=[tokens_vmem] * 3 + [pltpu.SemaphoreType.DMA((4,))],
            compiler_params=pltpu.CompilerParams(vmem_limit_bytes=32 * 1024 * 1024),
        )(*held)
        return (*grads, fgrad.T)

    return jax.shard_map(
        local,
        mesh=mesh,
        in_specs=(P("ctx", "ch"),) * 5 + (P("ctx"),),
        out_specs=(P("ctx", "ch"),) * 4,
        check_vma=False,
    )
```

time: 35.6 us -> 24.2 us (0.68)
  local copies, waits for them, and re-layouts: 5.91 us -> 0 us
  Pallas kernels: 28.8 us -> 23.4 us
    pallas_call x1 -> x2, Pallas kernels: 28.8 us -> 23.4 us  [the longest x1 22.6 us: local(): pl.pallas_call(partial(exchange_kernel, nz, nj, nf), out_shape=(turned, t...]
    unnamed x14 -> x0, local copies, waits for them, and re-layouts: 5.24 us -> none
    pallas_call x1 -> x0, local copies, waits for them, and re-layouts: 0.67 us -> none  [local(): pl.pallas_call(partial(kernel, nz, nj, nf), out_shape=(grad, grad, grad,...]
where the time goes in v2:
time: 24.2 us; the launch traced here: 24.1 us
  Pallas kernels  23.4 us (97%)
  between operations  0.64 us (3%)
    pallas_call x1, Pallas kernels, local(): pl.pallas_call(partial(exchange_kernel, nz, nj, nf), out_shape=(turned, t...  22.6 us
    pallas_call x1, Pallas kernels, local(): pl.pallas_call(gate_kernel, out_shape=(grad, grad, grad, jax.ShapeDtypeSt...  0.82 us

profile of v2, /device:TPU:1, one launch (start us, length us, event | category | flops | bytes accessed | tf_op | source)
XLA Modules:
  0.0 24.1 jit_solution(12540590289096525492)
XLA Ops:
  0.6 22.6 %shard_map.102 = (bf16[256,128]{1,0:T(8,128)(2,1)S(1)}, bf16[256,128]{1,0:T(8,128)(2,1)S(1)}, f32[16,128]{1,0:T(8,128)S(1)}, bf16[128,256]{1,0:T(8,128)(2,1)S(1)...) custom-call(s32[2]{0:T(128)} %ids_hbm.1, bf16[128,256]{1,0:T(8,128)(2,1)} %og_hbm.1, ...), custom_call_target="tpu_custom_call" | custom-call | tf_op jit(solution)/shard_map/pallas_call | solution.py:362
  23.2 0.8 %shard_map.103 = (bf16[128,256]{1,0:T(8,128)(2,1)}, bf16[128,256]{1,0:T(8,128)(2,1)}, bf16[128,256]{1,0:T(8,128)(2,1)}, f32[16,128]{1,0:T(8,128)}) custom-call(bf16[256,128]{1,0:T(8,128)(2,1)S(1)} %get-tuple-element.14.conv_ref, bf16[256,128]{1,0:T(8,128)(2,1)S(1)} %get-tuple-element.15.back_ref, f32[16,128]{1,0:T(8,128)S(1)} %get-tuple-element.16.fgrad_ref, ...), custom_call_target="tpu_custom_call" | custom-call | tf_op jit(solution)/shard_map/pallas_call | solution.py:404

commit v3 on v2

--- a/solution.py
+++ b/solution.py
@@ -67,6 +67,7 @@
     dft_ref,
     ids_ref,
     ids_all,
+    fl_ref,
     f_send,
     f_recv,
     a_send,
@@ -102,12 +103,12 @@
         pltpu.make_async_copy(src, dst, load_sems.at[k])
         for k, (src, dst) in enumerate(
             (
-                (fl_hbm, f_send),
                 (ig_hbm, ig_ref),
                 (sg_hbm, sg_ref),
                 (ct_hbm, ct_ref),
                 (og_hbm, og_ref),
                 (dft_hbm, dft_ref),
+                (fl_hbm, fl_ref),
                 (ids_hbm, ids_ref),
             )
         )
@@ -120,36 +121,57 @@
     def greet(device):
         pl.semaphore_signal(barrier, inc=1, device_id=device, device_id_type=MESH)
 
-    owners = [(lax.rem(zi + s, nz), 2 * mine + r) for s in range(nz) for r in range(2)]
+    def hops(step, size):
+        return min(step, size - step)
+
+    nd = nz // 2
+    steps = sorted(
+        ((dz, dc) for dz in range(nd) for dc in range(2)),
+        key=lambda s: (-hops(s[0], nd), -s[1]),
+    )
+    ctx_order = [2 * lax.rem(depth + dz, nd) + lax.rem(core + dc, 2) for dz, dc in steps]
+    group = ctx_order[:-1]
+    owners = [(z, 2 * mine + r) for z in ctx_order for r in range(2)]
     users = []
-    for s in range(nj):
-        j = lax.rem(ji + s, nj)
+    for dx, dy in sorted(
+        ((dx, dy) for dx in range(nx) for dy in range(4)),
+        key=lambda s: -hops(s[0], nx) - hops(s[1], 4),
+    ):
+        j = 4 * lax.rem(xi + dx, nx) + lax.rem(yi + dy, 4)
         users.append((user_of(j), j))
-    group = [lax.rem(zi + s, nz) for s in range(1, nz)]
     own = user_of(ji) == zi
+
+    def gray(value):
+        return value ^ (value >> 1)
+
+    rank = 2 * gray(depth) + 1 - core
+    first = [2 * gray(k // 2) + 1 - k % 2 for k in range(nz)]
+    urgent = [
+        jnp.where(rank <= k, first[k + 1], first[k]) for k in range(nz - 1)
+    ]
     own_side = [2 * mine + r == ji for r in range(2)]
 
+    for device in owners[:-2]:
+        greet(device)
     for r in range(2):
-        pl.when(jnp.logical_not(own_side[r]))(partial(greet, owners[r]))
-    for device in owners[2:]:
-        greet(device)
+        pl.when(jnp.logical_not(own_side[r]))(partial(greet, owners[r - 2]))
     for q in group:
         greet((q, ji))
-    pl.when(jnp.logical_not(own))(partial(greet, users[0]))
-    for device in users[1:]:
-        greet(device)
-
+    for step in range(1, nj):
+        greet((zi, lax.rem(ji + step, nj)))
+
+    loads[5].wait()
+    f_send[...] = fl_ref[...].astype(BF16)
     loads[0].wait()
     loads[1].wait()
-    loads[2].wait()
     product = ig_ref[...].astype(F32) * sg_ref[...].astype(F32)
     a_send[:, 0] = product.T.astype(BF16).reshape(nz, nc, SPAN)
+    loads[2].wait()
     loads[3].wait()
-    loads[4].wait()
     weighted = ct_ref[...].astype(F32) * og_ref[...].astype(F32)
     a_send[:, 1] = weighted.T.astype(BF16).reshape(nz, nc, SPAN)
 
-    pl.semaphore_wait(barrier, nz - 1 + 2 * nj - jnp.where(own, 2, 0))
+    pl.semaphore_wait(barrier, nz - 2 + 2 * nj - jnp.where(own, 1, 0))
 
     def remote(src, dst, k, device):
         return pltpu.make_async_remote_copy(
@@ -157,6 +179,8 @@
         )
 
     f_slot = f_recv.at[zi, yi % 2]
+    for device in users[:-1]:
+        remote(f_send, f_slot, 0, device).start()
 
     @pl.when(own)
     def _():
@@ -164,10 +188,7 @@
 
     @pl.when(jnp.logical_not(own))
     def _():
-        remote(f_send, f_slot, 0, users[0]).start()
-
-    for device in users[1:]:
-        remote(f_send, f_slot, 0, device).start()
+        remote(f_send, f_slot, 0, users[-1]).start()
 
     loads[6].wait()
     for q in group:
@@ -186,7 +207,7 @@
             place = jnp.where(ids[s] == n, s, place)
         order.append(place)
 
-    loads[5].wait()
+    loads[4].wait()
     table = dft_ref[...]
     low = iota((2 * nc, SPAN), 1) < HALF
     odd = iota((nc, FREQ), 1) % 2 == 1
@@ -237,28 +258,29 @@
     high, rest = split(jnp.concatenate(rows, axis=0))
     lags = mm_nt(high, table)
     lags = lags[:, :SPAN] + lags[:, SPAN:] + mm_nt(rest, table[:SPAN])
-    g_send[...] = (lags * (1.0 / SPAN)).reshape(nz, 2, nf, SPAN)
+    g_send[...] = (lags * (1.0 / SPAN)).astype(BF16).reshape(nz, 2, nf, SPAN)
 
     g_slot = g_recv.at[ji]
-    for r in range(2):
-        src = g_send.at[zi, r]
-
-        def keep(src=src):
-            pltpu.make_async_copy(src, g_slot, recv_sems.at[3]).start()
-
-        def pass_on(src=src, r=r):
-            remote(src, g_slot, 3, owners[r]).start()
-
-        pl.when(own_side[r])(keep)
-        pl.when(jnp.logical_not(own_side[r]))(pass_on)
-    for s in range(1, nz):
-        for r in range(2):
-            z, j = owners[2 * s + r]
-            remote(g_send.at[z, r], g_slot, 3, (z, j)).start()
+    near = ji % 2
+    for k in range(nz):
+        z = first[k]
+        remote(g_send.at[z, 1 - near], g_slot, 3, (z, 2 * mine + 1 - near)).start()
+        if k < nz - 1:
+            z = urgent[k]
+            remote(g_send.at[z, near], g_slot, 3, (z, 2 * mine + near)).start()
+
+    @pl.when(own)
+    def _():
+        pltpu.make_async_copy(g_send.at[zi, near], g_slot, recv_sems.at[3]).start()
+
+    @pl.when(jnp.logical_not(own))
+    def _():
+        remote(g_send.at[zi, near], g_slot, 3, (zi, 2 * mine + near)).start()
 
     wait_bytes(f_recv, 0, nz, recv_sems.at[0])
-    high, rest = split(f_recv[...].reshape(nz * nc, SPAN))
-    raw = mm(jnp.concatenate([high, high], axis=1), table) + mm(rest, table[:SPAN])
+
+    taps = f_recv[...].reshape(nz * nc, SPAN)
+    raw = mm(jnp.concatenate([taps, taps], axis=1), table)
     raw = raw.reshape(nz, nc, 2 * FREQ)
     for d in range(nz):
         re, im = raw[d, :, :FREQ], raw[d, :, FREQ:]
@@ -282,14 +304,14 @@
         spread(i, result[2 * nc * i : 2 * nc * (i + 1)])
     for z in range(nz):
         r_send[z] = pick(ids[2 * z], ids[2 * z + 1]).astype(BF16).reshape(2, nc, SPAN)
-    for q in group:
+    for q in urgent:
         remote(r_send.at[q], r_recv.at[mine], 4, (q, ji)).start()
     r_recv[mine] = r_send[zi]
 
     wait_bytes(g_recv, 0, nj, recv_sems.at[3])
-    total = g_recv[0]
+    total = g_recv[0].astype(F32)
     for j in range(1, nj):
-        total = total + g_recv[j]
+        total = total + g_recv[j].astype(F32)
     fgrad_ref[...] = total
 
     wait_bytes(r_recv, 0, nz - 1, recv_sems.at[4])
@@ -302,12 +324,12 @@
 
     @pl.when(own)
     def _():
-        wait_bytes(g_recv, 0, nj - 1, send_sems.at[0])
+        wait_bytes(f_recv.reshape(nj, nf, SPAN), 0, nj - 1, send_sems.at[0])
         wait_bytes(g_recv, 0, nj - 1, send_sems.at[3])
 
     @pl.when(jnp.logical_not(own))
     def _():
-        wait_bytes(g_recv, 0, nj, send_sems.at[0])
+        wait_bytes(f_recv, 0, nz, send_sems.at[0])
         wait_bytes(g_recv, 0, nj, send_sems.at[3])
 
 
@@ -370,13 +392,14 @@
                 pltpu.SMEM((2,), jnp.int32),
                 pltpu.SMEM((nz, 2), jnp.int32),
                 pltpu.VMEM((nf, SPAN), F32),
-                pltpu.VMEM((nz, 2, nf, SPAN), F32),
+                pltpu.VMEM((nf, SPAN), BF16),
+                pltpu.VMEM((nz, 2, nf, SPAN), BF16),
                 block,
                 block,
                 block,
                 block,
-                pltpu.VMEM((nz, 2, nf, SPAN), F32),
-                pltpu.VMEM((nj, nf, SPAN), F32),
+                pltpu.VMEM((nz, 2, nf, SPAN), BF16),
+                pltpu.VMEM((nj, nf, SPAN), BF16),
                 pltpu.VMEM((2 * nz, 2 * nc, SPAN), F32),
                 pltpu.VMEM((nz, 2, nc, 2 * FREQ), F32),
                 pltpu.VMEM((nz, nc, 2 * FREQ), F32),

time: 24.2 us -> 21.3 us (0.88)
  Pallas kernels: 23.4 us -> 20.5 us
    pallas_call x1, Pallas kernels: 22.6 us -> 19.7 us  [local(): pl.pallas_call(partial(exchange_kernel, nz, nj, nf), out_shape=(turned, t...]
where the time goes in v3:
time: 21.3 us; the launch traced here: 21.2 us
  Pallas kernels  20.5 us (96%)
  between operations  0.64 us (3%)
    pallas_call x1, Pallas kernels, local(): pl.pallas_call(partial(exchange_kernel, nz, nj, nf), out_shape=(turned, t...  19.7 us
    pallas_call x1, Pallas kernels, local(): pl.pallas_call(gate_kernel, out_shape=(grad, grad, grad, jax.ShapeDtypeSt...  0.82 us

profile of v3, /device:TPU:1, one launch (start us, length us, event | category | flops | bytes accessed | tf_op | source)
XLA Modules:
  0.0 21.2 jit_solution(9752244026502317817)
XLA Ops:
  0.6 19.7 %shard_map.102 = (bf16[256,128]{1,0:T(8,128)(2,1)S(1)}, bf16[256,128]{1,0:T(8,128)(2,1)S(1)}, f32[16,128]{1,0:T(8,128)S(1)}, bf16[128,256]{1,0:T(8,128)(2,1)S(1)...) custom-call(s32[2]{0:T(128)} %ids_hbm.1, bf16[128,256]{1,0:T(8,128)(2,1)} %og_hbm.1, ...), custom_call_target="tpu_custom_call" | custom-call | tf_op jit(solution)/shard_map/pallas_call | solution.py:384
  20.3 0.8 %shard_map.103 = (bf16[128,256]{1,0:T(8,128)(2,1)}, bf16[128,256]{1,0:T(8,128)(2,1)}, bf16[128,256]{1,0:T(8,128)(2,1)}, f32[16,128]{1,0:T(8,128)}) custom-call(bf16[256,128]{1,0:T(8,128)(2,1)S(1)} %get-tuple-element.14.conv_ref, bf16[256,128]{1,0:T(8,128)(2,1)S(1)} %get-tuple-element.15.back_ref, f32[16,128]{1,0:T(8,128)S(1)} %get-tuple-element.16.fgrad_ref, ...), custom_call_target="tpu_custom_call" | custom-call | tf_op jit(solution)/shard_map/pallas_call | solution.py:427

commit v4 on v3

--- a/solution.py
+++ b/solution.py
@@ -91,13 +91,57 @@
     xi, yi = ji // 4, ji % 4
 
     def chunk_of(q):
-        return 2 * lax.rem(xi + q // 2 + nx // 2, nx) + lax.rem(q + yi // 2, 2)
+        return 2 * lax.rem(xi + q // 2 + 1, nx) + lax.rem(q + yi // 2, 2)
 
     def user_of(j):
-        z = lax.rem(xi + nx - j // 4 + nx // 2, nx)
+        z = lax.rem(xi + 2 * nx - j // 4 - 1, nx)
         return 2 * z + lax.rem(yi // 2 + j % 4 // 2, 2)
 
     mine = chunk_of(zi)
+
+    barrier = pltpu.get_barrier_semaphore()
+
+    def greet(device):
+        pl.semaphore_signal(barrier, inc=1, device_id=device, device_id_type=MESH)
+
+    def hops(step, size):
+        return min(step, size - step)
+
+    nd = nz // 2
+    steps = sorted(
+        ((dz, dc) for dz in range(nd) for dc in range(2)),
+        key=lambda s: (-hops(s[0], nd), -s[1]),
+    )
+    ctx_order = [2 * lax.rem(depth + dz, nd) + lax.rem(core + dc, 2) for dz, dc in steps]
+    group = ctx_order[:-1]
+    owners = [(z, 2 * mine + r) for z in ctx_order for r in range(2)]
+    users = []
+    for dx, dy in sorted(
+        ((dx, dy) for dx in range(nx) for dy in range(4)),
+        key=lambda s: -hops(s[0], nx) - hops(s[1], 4),
+    ):
+        j = 4 * lax.rem(xi + dx, nx) + lax.rem(yi + dy, 4)
+        users.append((user_of(j), j))
+    own = user_of(ji) == zi
+
+    def gray(value):
+        return value ^ (value >> 1)
+
+    rank = 2 * gray(depth) + 1 - core
+    first = [2 * gray(k // 2) + 1 - k % 2 for k in range(nz)]
+    urgent = [
+        jnp.where(rank <= k, first[k + 1], first[k]) for k in range(nz - 1)
+    ]
+    own_side = [2 * mine + r == ji for r in range(2)]
+
+    for device in owners[:-2]:
+        greet(device)
+    for r in range(2):
+        pl.when(jnp.logical_not(own_side[r]))(partial(greet, owners[r - 2]))
+    for q in group:
+        greet((q, ji))
+    for step in range(1, nj):
+        greet((zi, lax.rem(ji + step, nj)))
 
     loads = [
         pltpu.make_async_copy(src, dst, load_sems.at[k])
@@ -116,50 +160,6 @@
     for load in loads:
         load.start()
 
-    barrier = pltpu.get_barrier_semaphore()
-
-    def greet(device):
-        pl.semaphore_signal(barrier, inc=1, device_id=device, device_id_type=MESH)
-
-    def hops(step, size):
-        return min(step, size - step)
-
-    nd = nz // 2
-    steps = sorted(
-        ((dz, dc) for dz in range(nd) for dc in range(2)),
-        key=lambda s: (-hops(s[0], nd), -s[1]),
-    )
-    ctx_order = [2 * lax.rem(depth + dz, nd) + lax.rem(core + dc, 2) for dz, dc in steps]
-    group = ctx_order[:-1]
-    owners = [(z, 2 * mine + r) for z in ctx_order for r in range(2)]
-    users = []
-    for dx, dy in sorted(
-        ((dx, dy) for dx in range(nx) for dy in range(4)),
-        key=lambda s: -hops(s[0], nx) - hops(s[1], 4),
-    ):
-        j = 4 * lax.rem(xi + dx, nx) + lax.rem(yi + dy, 4)
-        users.append((user_of(j), j))
-    own = user_of(ji) == zi
-
-    def gray(value):
-        return value ^ (value >> 1)
-
-    rank = 2 * gray(depth) + 1 - core
-    first = [2 * gray(k // 2) + 1 - k % 2 for k in range(nz)]
-    urgent = [
-        jnp.where(rank <= k, first[k + 1], first[k]) for k in range(nz - 1)
-    ]
-    own_side = [2 * mine + r == ji for r in range(2)]
-
-    for device in owners[:-2]:
-        greet(device)
-    for r in range(2):
-        pl.when(jnp.logical_not(own_side[r]))(partial(greet, owners[r - 2]))
-    for q in group:
-        greet((q, ji))
-    for step in range(1, nj):
-        greet((zi, lax.rem(ji + step, nj)))
-
     loads[5].wait()
     f_send[...] = fl_ref[...].astype(BF16)
     loads[0].wait()
@@ -179,21 +179,23 @@
         )
 
     f_slot = f_recv.at[zi, yi % 2]
-    for device in users[:-1]:
+    loads[6].wait()
+    for device in users[:5]:
         remote(f_send, f_slot, 0, device).start()
-
-    @pl.when(own)
-    def _():
-        pltpu.make_async_copy(f_send, f_slot, recv_sems.at[0]).start()
-
-    @pl.when(jnp.logical_not(own))
-    def _():
-        remote(f_send, f_slot, 0, users[-1]).start()
-
-    loads[6].wait()
     for q in group:
         remote(ids_ref, ids_all.at[zi], 1, (q, ji)).start()
         remote(a_send.at[chunk_of(q)], a_recv.at[zi], 2, (q, ji)).start()
+    for device in users[5:-1]:
+        remote(f_send, f_slot, 0, device).start()
+
+    @pl.when(own)
+    def _():
+        pltpu.make_async_copy(f_send, f_slot, recv_sems.at[0]).start()
+
+    @pl.when(jnp.logical_not(own))
+    def _():
+        remote(f_send, f_slot, 0, users[-1]).start()
+
     ids_all[zi, 0] = ids_ref[0]
     ids_all[zi, 1] = ids_ref[1]
     a_recv[zi] = a_send[mine]

time: 21.3 us -> 20.5 us (0.962)
  Pallas kernels: 20.5 us -> 19.7 us
    pallas_call x1, Pallas kernels: 19.7 us -> 18.9 us  [local(): pl.pallas_call(partial(exchange_kernel, nz, nj, nf), out_shape=(turned, t...]
where the time goes in v4:
time: 20.5 us; the launch traced here: 20.4 us
  Pallas kernels  19.7 us (96%)
  between operations  0.64 us (3%)
    pallas_call x1, Pallas kernels, local(): pl.pallas_call(partial(exchange_kernel, nz, nj, nf), out_shape=(turned, t...  18.9 us
    pallas_call x1, Pallas kernels, local(): pl.pallas_call(gate_kernel, out_shape=(grad, grad, grad, jax.ShapeDtypeSt...  0.82 us

profile of v4, /device:TPU:1, one launch (start us, length us, event | category | flops | bytes accessed | tf_op | source)
XLA Modules:
  0.0 20.4 jit_solution(14643720367357747244)
XLA Ops:
  0.6 18.9 %shard_map.102 = (bf16[256,128]{1,0:T(8,128)(2,1)S(1)}, bf16[256,128]{1,0:T(8,128)(2,1)S(1)}, f32[16,128]{1,0:T(8,128)S(1)}, bf16[128,256]{1,0:T(8,128)(2,1)S(1)...) custom-call(s32[2]{0:T(128)} %ids_hbm.1, bf16[128,256]{1,0:T(8,128)(2,1)} %og_hbm.1, ...), custom_call_target="tpu_custom_call" | custom-call | tf_op jit(solution)/shard_map/pallas_call | solution.py:386
  19.5 0.8 %shard_map.103 = (bf16[128,256]{1,0:T(8,128)(2,1)}, bf16[128,256]{1,0:T(8,128)(2,1)}, bf16[128,256]{1,0:T(8,128)(2,1)}, f32[16,128]{1,0:T(8,128)}) custom-call(bf16[256,128]{1,0:T(8,128)(2,1)S(1)} %get-tuple-element.14.conv_ref, bf16[256,128]{1,0:T(8,128)(2,1)S(1)} %get-tuple-element.15.back_ref, f32[16,128]{1,0:T(8,128)S(1)} %get-tuple-element.16.fgrad_ref, ...), custom_call_target="tpu_custom_call" | custom-call | tf_op jit(solution)/shard_map/pallas_call | solution.py:429

commit v5 on v4

--- a/solution.py
+++ b/solution.py
@@ -28,12 +28,22 @@
     return np.concatenate([high, low], axis=0)
 
 
-def mm(left, right):
-    return jnp.dot(left, right, preferred_element_type=F32)
+def mm(left, right, nt=False, parts=4):
+    dims = (((1,), (1 if nt else 0,)), ((), ()))
+    step = left.shape[0] // parts
+    return jnp.concatenate(
+        [
+            lax.dot_general(
+                left[k * step : (k + 1) * step], right, dims, preferred_element_type=F32
+            )
+            for k in range(parts)
+        ],
+        axis=0,
+    )
 
 
 def mm_nt(left, right):
-    return lax.dot_general(left, right, (((1,), (1,)), ((), ())), preferred_element_type=F32)
+    return mm(left, right, nt=True)
 
 
 def wait_bytes(ref, start, count, sem):
@@ -79,6 +89,7 @@
     halves,
     spec,
     wspec,
+    sums,
     load_sems,
     send_sems,
     recv_sems,
@@ -180,12 +191,12 @@
 
     f_slot = f_recv.at[zi, yi % 2]
     loads[6].wait()
-    for device in users[:5]:
+    for device in users[: nj // 4]:
         remote(f_send, f_slot, 0, device).start()
     for q in group:
         remote(ids_ref, ids_all.at[zi], 1, (q, ji)).start()
         remote(a_send.at[chunk_of(q)], a_recv.at[zi], 2, (q, ji)).start()
-    for device in users[5:-1]:
+    for device in users[nj // 4 : -1]:
         remote(f_send, f_slot, 0, device).start()
 
     @pl.when(own)
@@ -212,8 +223,7 @@
     loads[4].wait()
     table = dft_ref[...]
     low = iota((2 * nc, SPAN), 1) < HALF
-    odd = iota((nc, FREQ), 1) % 2 == 1
-    sign = jnp.where(odd, -1.0, 1.0)
+    sign = jnp.where(iota((8, FREQ), 1) % 2 == 1, -1.0, 1.0)
 
     def spread(slot, values):
         turned = pltpu.roll(values, HALF, 1)
@@ -232,9 +242,14 @@
         nz, 2, nc, 2 * FREQ
     )
 
-    def part(ref, *at):
-        value = ref[at]
-        return value[:, :FREQ], value[:, FREQ:]
+    groups = [slice(k, k + 8) for k in range(0, nc, 8)]
+
+    def load(ref, *at):
+        return ref[(*at, slice(0, FREQ))], ref[(*at, slice(FREQ, 2 * FREQ))]
+
+    def store(ref, value, *at):
+        ref[(*at, slice(0, FREQ))] = value[0]
+        ref[(*at, slice(FREQ, 2 * FREQ))] = value[1]
 
     def times(total, left, right):
         (a, b), (c, d) = left, right
@@ -246,18 +261,22 @@
         re, im = a * c + b * d, a * d - b * c
         return (re, im) if total is None else (total[0] + re, total[1] + im)
 
-    cross = [None] * (nz + 1)
-    for d in range(nz):
-        for i in range(nz - d):
-            cross[d] = against(cross[d], part(spec, i, 0), part(spec, i + d, 1))
-    rows = []
-    for d in range(nz):
-        re, im = cross[d]
-        if d + 1 < nz:
-            re = re + sign * cross[d + 1][1]
-            im = im - sign * cross[d + 1][0]
-        rows.append(jnp.concatenate([re, im], axis=1))
-    high, rest = split(jnp.concatenate(rows, axis=0))
+    for at in groups:
+        left = [load(spec, i, 0, at) for i in range(nz)]
+        right = [load(spec, i, 1, at) for i in range(nz)]
+        cross = []
+        for d in range(nz):
+            total = None
+            for i in range(nz - d):
+                total = against(total, left[i], right[i + d])
+            cross.append(total)
+        for d in range(nz):
+            re, im = cross[d]
+            if d + 1 < nz:
+                re = re + sign * cross[d + 1][1]
+                im = im - sign * cross[d + 1][0]
+            store(wspec, (re, im), d, at)
+    high, rest = split(wspec[...].reshape(nz * nc, 2 * FREQ))
     lags = mm_nt(high, table)
     lags = lags[:, :SPAN] + lags[:, SPAN:] + mm_nt(rest, table[:SPAN])
     g_send[...] = (lags * (1.0 / SPAN)).astype(BF16).reshape(nz, 2, nf, SPAN)
@@ -283,25 +302,28 @@
 
     taps = f_recv[...].reshape(nz * nc, SPAN)
     raw = mm(jnp.concatenate([taps, taps], axis=1), table)
-    raw = raw.reshape(nz, nc, 2 * FREQ)
-    for d in range(nz):
-        re, im = raw[d, :, :FREQ], raw[d, :, FREQ:]
-        if d:
-            re = re - sign * raw[d - 1, :, FREQ:]
-            im = im + sign * raw[d - 1, :, :FREQ]
-        wspec[d, :, :FREQ] = re
-        wspec[d, :, FREQ:] = im
-
-    rows = []
-    for m in range(nz):
-        conv = back = None
-        for i in range(m + 1):
-            conv = times(conv, part(wspec, m - i), part(spec, i, 0))
-        for j in range(m, nz):
-            back = against(back, part(wspec, j - m), part(spec, j, 1))
-        rows += [jnp.concatenate(conv, axis=1), jnp.concatenate(back, axis=1)]
-    result = mm_nt(jnp.concatenate(rows, axis=0).astype(BF16), table)
-    result = (result[:, :SPAN] + result[:, SPAN:]) * (1.0 / SPAN)
+    wspec[...] = raw.reshape(nz, nc, 2 * FREQ)
+    for at in groups:
+        taps = [load(wspec, d, at) for d in range(nz)]
+        for d in reversed(range(1, nz)):
+            (re, im), (before_re, before_im) = taps[d], taps[d - 1]
+            taps[d] = (re - sign * before_im, im + sign * before_re)
+        left = [load(spec, i, 0, at) for i in range(nz)]
+        for m in range(nz):
+            total = None
+            for i in range(m + 1):
+                total = times(total, taps[m - i], left[i])
+            store(sums, total, m, 0, at)
+        right = [load(spec, i, 1, at) for i in range(nz)]
+        for m in range(nz):
+            total = None
+            for j in range(m, nz):
+                total = against(total, taps[j - m], right[j])
+            store(sums, total, m, 1, at)
+    high, rest = split(sums[...].reshape(2 * nz * nc, 2 * FREQ))
+    result = mm_nt(high, table)
+    result = result[:, :SPAN] + result[:, SPAN:] + mm_nt(rest, table[:SPAN])
+    result = result * (1.0 / SPAN)
     for i in range(nz):
         spread(i, result[2 * nc * i : 2 * nc * (i + 1)])
     for z in range(nz):
@@ -405,6 +427,7 @@
                 pltpu.VMEM((2 * nz, 2 * nc, SPAN), F32),
                 pltpu.VMEM((nz, 2, nc, 2 * FREQ), F32),
                 pltpu.VMEM((nz, nc, 2 * FREQ), F32),
+                pltpu.VMEM((nz, 2, nc, 2 * FREQ), F32),
                 pltpu.SemaphoreType.DMA((7,)),
                 pltpu.SemaphoreType.DMA((5,)),
                 pltpu.SemaphoreType.DMA((5,)),

time: 20.5 us -> 20.6 us (level)
  no operation moved by 1% of the time
where the time goes in v5:
time: 20.6 us; the launch traced here: 20.5 us
  Pallas kernels  19.8 us (96%)
  between operations  0.64 us (3%)
    pallas_call x1, Pallas kernels, local(): pl.pallas_call(partial(exchange_kernel, nz, nj, nf), out_shape=(turned, t...  19 us
    pallas_call x1, Pallas kernels, local(): pl.pallas_call(gate_kernel, out_shape=(grad, grad, grad, jax.ShapeDtypeSt...  0.82 us

profile of v5, /device:TPU:1, one launch (start us, length us, event | category | flops | bytes accessed | tf_op | source)
XLA Modules:
  0.0 20.5 jit_solution(15508950299997556987)
XLA Ops:
  0.6 19.0 %shard_map.102 = (bf16[256,128]{1,0:T(8,128)(2,1)S(1)}, bf16[256,128]{1,0:T(8,128)(2,1)S(1)}, f32[16,128]{1,0:T(8,128)S(1)}, bf16[128,256]{1,0:T(8,128)(2,1)S(1)...) custom-call(s32[2]{0:T(128)} %ids_hbm.1, bf16[128,256]{1,0:T(8,128)(2,1)} %og_hbm.1, ...), custom_call_target="tpu_custom_call" | custom-call | tf_op jit(solution)/shard_map/pallas_call | solution.py:408
  19.6 0.8 %shard_map.103 = (bf16[128,256]{1,0:T(8,128)(2,1)}, bf16[128,256]{1,0:T(8,128)(2,1)}, bf16[128,256]{1,0:T(8,128)(2,1)}, f32[16,128]{1,0:T(8,128)}) custom-call(bf16[256,128]{1,0:T(8,128)(2,1)S(1)} %get-tuple-element.14.conv_ref, bf16[256,128]{1,0:T(8,128)(2,1)S(1)} %get-tuple-element.15.back_ref, f32[16,128]{1,0:T(8,128)S(1)} %get-tuple-element.16.fgrad_ref, ...), custom_call_target="tpu_custom_call" | custom-call | tf_op jit(solution)/shard_map/pallas_call | solution.py:452

commit v6 on v5

--- a/solution.py
+++ b/solution.py
@@ -28,32 +28,17 @@
     return np.concatenate([high, low], axis=0)
 
 
-def mm(left, right, nt=False, parts=4):
-    dims = (((1,), (1 if nt else 0,)), ((), ()))
-    step = left.shape[0] // parts
-    return jnp.concatenate(
-        [
-            lax.dot_general(
-                left[k * step : (k + 1) * step], right, dims, preferred_element_type=F32
-            )
-            for k in range(parts)
-        ],
-        axis=0,
-    )
+def mm(left, right):
+    return jnp.dot(left, right, preferred_element_type=F32)
 
 
 def mm_nt(left, right):
-    return mm(left, right, nt=True)
+    return lax.dot_general(left, right, (((1,), (1,)), ((), ())), preferred_element_type=F32)
 
 
 def wait_bytes(ref, start, count, sem):
     view = ref.at[pl.ds(start, count)]
     pltpu.make_async_copy(view, view, sem).wait()
-
-
-def split(values):
-    high = values.astype(BF16)
-    return high, (values - high.astype(F32)).astype(BF16)
 
 
 def exchange_kernel(
@@ -89,7 +74,6 @@
     halves,
     spec,
     wspec,
-    sums,
     load_sems,
     send_sems,
     recv_sems,
@@ -227,11 +211,12 @@
 
     def spread(slot, values):
         turned = pltpu.roll(values, HALF, 1)
-        halves[2 * slot] = jnp.where(low, values, turned)
-        halves[2 * slot + 1] = jnp.where(low, turned, values)
+        halves[2 * slot] = jnp.where(low, values, turned).reshape(2, nc, SPAN)
+        halves[2 * slot + 1] = jnp.where(low, turned, values).reshape(2, nc, SPAN)
 
     def pick(first, second):
-        return jnp.where(low, halves[first], halves[second])
+        first, second = (halves[k].reshape(2 * nc, SPAN) for k in (first, second))
+        return jnp.where(low, first, second)
 
     wait_bytes(a_recv, 0, nz - 1, recv_sems.at[2])
     for z in range(nz):
@@ -247,9 +232,10 @@
     def load(ref, *at):
         return ref[(*at, slice(0, FREQ))], ref[(*at, slice(FREQ, 2 * FREQ))]
 
-    def store(ref, value, *at):
-        ref[(*at, slice(0, FREQ))] = value[0]
-        ref[(*at, slice(FREQ, 2 * FREQ))] = value[1]
+    def inverse(parts):
+        rows = jnp.concatenate([jnp.concatenate(part, axis=1) for part in parts], axis=0)
+        points = mm_nt(rows.astype(BF16), table)
+        return (points[:, :SPAN] + points[:, SPAN:]) * (1.0 / SPAN)
 
     def times(total, left, right):
         (a, b), (c, d) = left, right
@@ -261,25 +247,26 @@
         re, im = a * c + b * d, a * d - b * c
         return (re, im) if total is None else (total[0] + re, total[1] + im)
 
-    for at in groups:
-        left = [load(spec, i, 0, at) for i in range(nz)]
-        right = [load(spec, i, 1, at) for i in range(nz)]
-        cross = []
-        for d in range(nz):
-            total = None
-            for i in range(nz - d):
-                total = against(total, left[i], right[i + d])
-            cross.append(total)
-        for d in range(nz):
-            re, im = cross[d]
-            if d + 1 < nz:
-                re = re + sign * cross[d + 1][1]
-                im = im - sign * cross[d + 1][0]
-            store(wspec, (re, im), d, at)
-    high, rest = split(wspec[...].reshape(nz * nc, 2 * FREQ))
-    lags = mm_nt(high, table)
-    lags = lags[:, :SPAN] + lags[:, SPAN:] + mm_nt(rest, table[:SPAN])
-    g_send[...] = (lags * (1.0 / SPAN)).astype(BF16).reshape(nz, 2, nf, SPAN)
+    for r in range(2):
+        parts = [[None, None] for _ in range(nz)]
+        for k in range(2):
+            at = groups[2 * r + k]
+            left = [load(spec, i, 0, at) for i in range(nz)]
+            right = [load(spec, i, 1, at) for i in range(nz)]
+            cross = []
+            for d in range(nz):
+                total = None
+                for i in range(nz - d):
+                    total = against(total, left[i], right[i + d])
+                cross.append(total)
+            for d in range(nz):
+                re, im = cross[d]
+                if d + 1 < nz:
+                    re = re + sign * cross[d + 1][1]
+                    im = im - sign * cross[d + 1][0]
+                parts[d][k] = (re, im)
+        lags = inverse([part for pair in parts for part in pair])
+        g_send[:, r] = lags.astype(BF16).reshape(nz, nf, SPAN)
 
     g_slot = g_recv.at[ji]
     near = ji % 2
@@ -308,24 +295,28 @@
         for d in reversed(range(1, nz)):
             (re, im), (before_re, before_im) = taps[d], taps[d - 1]
             taps[d] = (re - sign * before_im, im + sign * before_re)
+        parts = []
         left = [load(spec, i, 0, at) for i in range(nz)]
         for m in range(nz):
             total = None
             for i in range(m + 1):
                 total = times(total, taps[m - i], left[i])
-            store(sums, total, m, 0, at)
+            parts.append(total)
         right = [load(spec, i, 1, at) for i in range(nz)]
         for m in range(nz):
             total = None
             for j in range(m, nz):
                 total = against(total, taps[j - m], right[j])
-            store(sums, total, m, 1, at)
-    high, rest = split(sums[...].reshape(2 * nz * nc, 2 * FREQ))
-    result = mm_nt(high, table)
-    result = result[:, :SPAN] + result[:, SPAN:] + mm_nt(rest, table[:SPAN])
-    result = result * (1.0 / SPAN)
-    for i in range(nz):
-        spread(i, result[2 * nc * i : 2 * nc * (i + 1)])
+            parts.append(total)
+        points = inverse(parts)
+        low8 = iota((8, SPAN), 1) < HALF
+        for i in range(nz):
+            for kind in range(2):
+                row = 8 * (kind * nz + i)
+                block = points[row : row + 8]
+                turned = pltpu.roll(block, HALF, 1)
+                halves[2 * i, kind, at] = jnp.where(low8, block, turned)
+                halves[2 * i + 1, kind, at] = jnp.where(low8, turned, block)
     for z in range(nz):
         r_send[z] = pick(ids[2 * z], ids[2 * z + 1]).astype(BF16).reshape(2, nc, SPAN)
     for q in urgent:
@@ -424,10 +415,9 @@
                 block,
                 pltpu.VMEM((nz, 2, nf, SPAN), BF16),
                 pltpu.VMEM((nj, nf, SPAN), BF16),
-                pltpu.VMEM((2 * nz, 2 * nc, SPAN), F32),
+                pltpu.VMEM((2 * nz, 2, nc, SPAN), F32),
                 pltpu.VMEM((nz, 2, nc, 2 * FREQ), F32),
                 pltpu.VMEM((nz, nc, 2 * FREQ), F32),
-                pltpu.VMEM((nz, 2, nc, 2 * FREQ), F32),
                 pltpu.SemaphoreType.DMA((7,)),
                 pltpu.SemaphoreType.DMA((5,)),
                 pltpu.SemaphoreType.DMA((5,)),

time: 20.6 us -> 20.4 us (level)
  no operation moved by 1% of the time
where the time goes in v6:
time: 20.4 us; the launch traced here: 20.3 us
  Pallas kernels  19.7 us (97%)
  between operations  0.64 us (3%)
    pallas_call x1, Pallas kernels, local(): pl.pallas_call(partial(exchange_kernel, nz, nj, nf), out_shape=(turned, t...  18.9 us
    pallas_call x1, Pallas kernels, local(): pl.pallas_call(gate_kernel, out_shape=(grad, grad, grad, jax.ShapeDtypeSt...  0.82 us

profile of v6, /device:TPU:1, one launch (start us, length us, event | category | flops | bytes accessed | tf_op | source)
XLA Modules:
  0.0 20.3 jit_solution(18013235339856572612)
XLA Ops:
  0.6 18.9 %shard_map.102 = (bf16[256,128]{1,0:T(8,128)(2,1)S(1)}, bf16[256,128]{1,0:T(8,128)(2,1)S(1)}, f32[16,128]{1,0:T(8,128)S(1)}, bf16[128,256]{1,0:T(8,128)(2,1)S(1)...) custom-call(s32[2]{0:T(128)} %ids_hbm.1, bf16[128,256]{1,0:T(8,128)(2,1)} %og_hbm.1, ...), custom_call_target="tpu_custom_call" | custom-call | tf_op jit(solution)/shard_map/pallas_call | solution.py:399
  19.5 0.8 %shard_map.103 = (bf16[128,256]{1,0:T(8,128)(2,1)}, bf16[128,256]{1,0:T(8,128)(2,1)}, bf16[128,256]{1,0:T(8,128)(2,1)}, f32[16,128]{1,0:T(8,128)}) custom-call(bf16[256,128]{1,0:T(8,128)(2,1)S(1)} %get-tuple-element.14.conv_ref, bf16[256,128]{1,0:T(8,128)(2,1)S(1)} %get-tuple-element.15.back_ref, f32[16,128]{1,0:T(8,128)S(1)} %get-tuple-element.16.fgrad_ref, ...), custom_call_target="tpu_custom_call" | custom-call | tf_op jit(solution)/shard_map/pallas_call | solution.py:442

commit v7 on v6

--- a/solution.py
+++ b/solution.py
@@ -173,12 +173,16 @@
             src, dst, send_sems.at[k], recv_sems.at[k], device, MESH
         )
 
+    loads[6].wait()
+    for q in group:
+        remote(ids_ref, ids_all.at[zi], 1, (q, ji)).start()
+    ids_all[zi, 0] = ids_ref[0]
+    ids_all[zi, 1] = ids_ref[1]
+
     f_slot = f_recv.at[zi, yi % 2]
-    loads[6].wait()
     for device in users[: nj // 4]:
         remote(f_send, f_slot, 0, device).start()
     for q in group:
-        remote(ids_ref, ids_all.at[zi], 1, (q, ji)).start()
         remote(a_send.at[chunk_of(q)], a_recv.at[zi], 2, (q, ji)).start()
     for device in users[nj // 4 : -1]:
         remote(f_send, f_slot, 0, device).start()
@@ -191,18 +195,19 @@
     def _():
         remote(f_send, f_slot, 0, users[-1]).start()
 
-    ids_all[zi, 0] = ids_ref[0]
-    ids_all[zi, 1] = ids_ref[1]
     a_recv[zi] = a_send[mine]
 
     wait_bytes(ids_all, 0, nz - 1, recv_sems.at[1])
     ids = [ids_all[s // 2, s % 2] for s in range(2 * nz)]
-    order = []
-    for n in range(2 * nz):
-        place = jnp.int32(0)
-        for s in range(2 * nz):
-            place = jnp.where(ids[s] == n, s, place)
-        order.append(place)
+    low_word = high_word = jnp.int32(0)
+    for s in range(1, 2 * nz):
+        place = s << (4 * (ids[s] & 7))
+        low_word = low_word + jnp.where(ids[s] < 8, place, 0)
+        high_word = high_word + jnp.where(ids[s] < 8, 0, place)
+    order = [
+        lax.shift_right_logical(low_word if n < 8 else high_word, jnp.int32(4 * (n % 8))) & 15
+        for n in range(2 * nz)
+    ]
 
     loads[4].wait()
     table = dft_ref[...]

time: 20.4 us -> 20.5 us (level)
  no operation moved by 1% of the time
where the time goes in v7:
time: 20.5 us; the launch traced here: 20.4 us
  Pallas kernels  19.7 us (96%)
  between operations  0.64 us (3%)
    pallas_call x1, Pallas kernels, local(): pl.pallas_call(partial(exchange_kernel, nz, nj, nf), out_shape=(turned, t...  18.9 us
    pallas_call x1, Pallas kernels, local(): pl.pallas_call(gate_kernel, out_shape=(grad, grad, grad, jax.ShapeDtypeSt...  0.82 us

profile of v7, /device:TPU:1, one launch (start us, length us, event | category | flops | bytes accessed | tf_op | source)
XLA Modules:
  0.0 20.4 jit_solution(11768527749178611362)
XLA Ops:
  0.6 18.9 %shard_map.102 = (bf16[256,128]{1,0:T(8,128)(2,1)S(1)}, bf16[256,128]{1,0:T(8,128)(2,1)S(1)}, f32[16,128]{1,0:T(8,128)S(1)}, bf16[128,256]{1,0:T(8,128)(2,1)S(1)...) custom-call(s32[2]{0:T(128)} %ids_hbm.1, bf16[128,256]{1,0:T(8,128)(2,1)} %og_hbm.1, ...), custom_call_target="tpu_custom_call" | custom-call | tf_op jit(solution)/shard_map/pallas_call | solution.py:404
  19.5 0.8 %shard_map.103 = (bf16[128,256]{1,0:T(8,128)(2,1)}, bf16[128,256]{1,0:T(8,128)(2,1)}, bf16[128,256]{1,0:T(8,128)(2,1)}, f32[16,128]{1,0:T(8,128)}) custom-call(bf16[256,128]{1,0:T(8,128)(2,1)S(1)} %get-tuple-element.14.conv_ref, bf16[256,128]{1,0:T(8,128)(2,1)S(1)} %get-tuple-element.15.back_ref, f32[16,128]{1,0:T(8,128)S(1)} %get-tuple-element.16.fgrad_ref, ...), custom_call_target="tpu_custom_call" | custom-call | tf_op jit(solution)/shard_map/pallas_call | solution.py:447
